TPU v7x, 128 devices: a whole 4x4x4 slice. The times are simulated.
128 devices in a mesh: gy: 8 (over y, core), gx: 16 (over x, z).
Axes of the slice: x: 4, y: 4, z: 4, core: 2. Of those that a mesh axis runs over, the one named last changes fastest.
Arguments:
- features: bfloat16 [1024, 512, 128], P(('gy', 'gx')), may hold values from -6 to 6
- links: int32 [1024, 3], P(('gy', 'gx')), may hold values 0 or 1
- block_slot: int32 [1024], P(('gy', 'gx')), may hold values from 0 to 31, as said below
- block_level: int32 [1024], P(('gy', 'gx')), may hold values from 0 to 3
- slot_column: int32 [128, 32], P(('gy', 'gx')), may hold values from 0 to 31
- conv_first: bfloat16 [7, 128, 128], replicated, may hold values from -0.1875 to 0.1875
- conv_second: bfloat16 [7, 128, 128], replicated, may hold values from -0.1875 to 0.1875
- height_w: bfloat16 [4, 1024, 256], replicated, may hold values from -0.1875 to 0.1875
- plane_first: bfloat16 [3, 3, 256, 256], replicated, may hold values from -0.125 to 0.125
- plane_second: bfloat16 [3, 3, 256, 256], replicated, may hold values from -0.125 to 0.125
Outputs:
- bev_out: bfloat16 [512, 512, 256], P('gy', 'gx')
Inputs may be any that keep to these rules, and one draw needn't show every extreme that they name: No two blocks of one device have both the same block_slot and the same block_level. At most 4 blocks of one device have the same block_slot // 2, and every device has exactly 4 such blocks for some value.
All inputs are finite; a program needn't handle non-finite values. No bound on the sum of `links` on one device may be relied on, other than what follows from the above.
Results may differ from a plain program's by a relative error of at most 0.0065.
Values may be sent and summed in bfloat16 or wider, within the bound.
A program may use at most 64 MiB of HBM per device.

v0:
```python
import jax
import jax.numpy as jnp
from jax import lax
from jax.sharding import PartitionSpec as P

EDGE = 8
STRIDE_Y = 8
TILE_BR = 8
TILE_BC = 4


def from_behind(block, axis, distance):
    devices = range(lax.axis_size(axis))
    route = [(i - distance, i) for i in devices if i - distance in devices]
    return lax.ppermute(block, axis, route)


def padded_2(cells, sides, width):
    for axis, dim in sides:
        count = lax.axis_size(axis)
        ends = count - 1
        head = lax.slice_in_dim(cells, 0, width, axis=dim)
        tail = lax.slice_in_dim(cells, cells.shape[dim] - width, cells.shape[dim], axis=dim)
        cells = jnp.concatenate(
            [
                lax.ppermute(tail, axis, [(i, (i + 1) % count) for i in range(ends)]),
                cells,
                lax.ppermute(head, axis, [((i + 1) % count, i) for i in range(ends)]),
            ],
            axis=dim,
        )
    return cells


def block_ghosts(blocks, links):
    block_count = blocks.shape[0]
    strides = (1, STRIDE_Y, block_count)
    uppers = []
    lowers = []
    keepers = []
    for axis_num in range(3):
        upper = lax.index_in_dim(blocks, EDGE - 1, axis_num + 1, keepdims=False)
        lower = lax.index_in_dim(blocks, 0, axis_num + 1, keepdims=False)
        keeping = links[:, axis_num].astype(blocks.dtype)[:, None, None, None]
        uppers.append(upper * keeping)
        lowers.append(lower)
        keepers.append(keeping)
    outgoing = [uppers[axis_num][block_count - strides[axis_num] :] for axis_num in range(3)]
    returning = [lowers[axis_num][: strides[axis_num]] for axis_num in range(3)]
    from_below = from_behind((outgoing[0], outgoing[1], outgoing[2]), ("gy", "gx"), 1)
    from_above = from_behind((returning[0], returning[1], returning[2]), ("gy", "gx"), -1)
    ghost_plus = []
    ghost_minus = []
    for axis_num in range(3):
        stride = strides[axis_num]
        ghost_plus.append(
            jnp.concatenate([lowers[axis_num][stride:], from_above[axis_num]], 0)
            * keepers[axis_num]
        )
        ghost_minus.append(
            jnp.concatenate([from_below[axis_num], uppers[axis_num][: block_count - stride]], 0)
        )
    return (ghost_plus, ghost_minus)


def seven_taps(blocks, ghost_plus, ghost_minus, weights):
    channels = blocks.shape[-1]
    result = jnp.dot(blocks.reshape(-1, channels), weights[0], preferred_element_type=jnp.float32)
    for axis_num in range(3):
        axis = axis_num + 1
        upward = jnp.concatenate(
            [
                lax.slice_in_dim(blocks, 1, EDGE, axis=axis),
                jnp.expand_dims(ghost_plus[axis_num], axis),
            ],
            axis,
        )
        downward = jnp.concatenate(
            [
                jnp.expand_dims(ghost_minus[axis_num], axis),
                lax.slice_in_dim(blocks, 0, EDGE - 1, axis=axis),
            ],
            axis,
        )
        result = result + jnp.dot(
            upward.reshape(-1, channels),
            weights[1 + 2 * axis_num],
            preferred_element_type=jnp.float32,
        )
        result = result + jnp.dot(
            downward.reshape(-1, channels),
            weights[2 + 2 * axis_num],
            preferred_element_type=jnp.float32,
        )
    return result.reshape(blocks.shape)


def plane_conv(padded, kernel, rows_out, cols_out):
    result = jnp.zeros((rows_out * cols_out, kernel.shape[3]), jnp.float32)
    for row_off in range(3):
        for col_off in range(3):
            window = padded[row_off : row_off + rows_out, col_off : col_off + cols_out].reshape(
                rows_out * cols_out, -1
            )
            result = result + jnp.dot(
                window, kernel[row_off, col_off], preferred_element_type=jnp.float32
            )
    return result.reshape(rows_out, cols_out, -1)


def tile_rim(plane):
    return padded_2(plane, (("gy", 0), ("gx", 1)), 1)


def local(
    features,
    links,
    block_slot,
    block_level,
    slot_column,
    conv_first,
    conv_second,
    height_w,
    plane_first,
    plane_second,
):
    block_count = features.shape[0]
    channels = features.shape[2]
    blocks = features.reshape(block_count, EDGE, EDGE, EDGE, channels)
    ghost_plus, ghost_minus = block_ghosts(blocks, links)
    hidden = jax.nn.relu(seven_taps(blocks, ghost_plus, ghost_minus, conv_first)).astype(
        jnp.bfloat16
    )
    ghost_plus, ghost_minus = block_ghosts(hidden, links)
    voxel = jax.nn.relu(
        blocks.astype(jnp.float32) + seven_taps(hidden, ghost_plus, ghost_minus, conv_second)
    ).astype(jnp.bfloat16)
    peer_count = lax.axis_size("gx")
    slot_total = slot_column.shape[1]
    per_peer = slot_total // peer_count
    rows_in = voxel.reshape(block_count, EDGE * EDGE, EDGE * channels)
    column_total = TILE_BR * TILE_BC
    chosen = jnp.take(height_w, block_level, axis=0)
    lifted = jnp.einsum("bpk,bkn->bpn", rows_in, chosen, preferred_element_type=jnp.float32)
    slot_pick = (block_slot[None, :] == jnp.arange(slot_total, dtype=jnp.int32)[:, None]).astype(
        jnp.float32
    )
    summed = jnp.dot(
        slot_pick,
        lifted.reshape(block_count, -1),
        precision=lax.Precision.HIGHEST,
        preferred_element_type=jnp.float32,
    )
    column_ids = slot_column.reshape(peer_count, per_peer).astype(jnp.float32)
    arrived_sums, arrived_ids = (
        lax.all_to_all(
            summed.reshape(peer_count, per_peer, -1), "gx", split_axis=0, concat_axis=0, tiled=True
        ),
        lax.all_to_all(column_ids, "gx", split_axis=0, concat_axis=0, tiled=True),
    )
    arrived_sums = arrived_sums.reshape(slot_total, -1)
    arrived_ids = arrived_ids.reshape(1, slot_total)
    column_map = (arrived_ids == jnp.arange(column_total, dtype=jnp.float32)[:, None]).astype(
        jnp.float32
    )
    tile_sum = jnp.dot(
        column_map,
        arrived_sums,
        precision=lax.Precision.HIGHEST,
        preferred_element_type=jnp.float32,
    )
    tile_rows = TILE_BR * EDGE
    tile_cols = TILE_BC * EDGE
    bev = tile_sum.reshape(TILE_BR, TILE_BC, EDGE, EDGE, -1).transpose(0, 2, 1, 3, 4)
    bev = bev.reshape(tile_rows, tile_cols, -1).astype(jnp.bfloat16)
    first = jax.nn.relu(plane_conv(tile_rim(bev), plane_first, tile_rows, tile_cols)).astype(
        jnp.bfloat16
    )
    second = plane_conv(tile_rim(first), plane_second, tile_rows, tile_cols)
    return (second + bev.astype(jnp.float32)).astype(jnp.bfloat16)


def solution(mesh):
    in_specs = (
        P(("gy", "gx"), None, None),
        P(("gy", "gx"), None),
        P(("gy", "gx")),
        P(("gy", "gx")),
        P(("gy", "gx"), None),
        P(),
        P(),
        P(),
        P(),
        P(),
    )
    out_specs = P("gy", "gx", None)
    return jax.shard_map(local, mesh=mesh, in_specs=in_specs, out_specs=out_specs, check_vma=False)
```

profile of v0, /device:TPU:1, one launch (start us, length us, event | category | flops | bytes accessed | tf_op | source)
XLA Modules:
  0.0 198.3 jit_solution(12576740076742630234)
XLA Ops:
  1.5 8.4 %all-to-all-start = ((f32[16,1,2]{2,1,0:T(1,128)}), f32[16,1,2]{2,1,0:T(1,128)S(1)}, u32[]{:S(2)}, u32[]{:S(2)}) async-start(f32[16,1,2]{2,1,0:T(1,128)} %bitcast), calls=%async_computation | async-start | bytes 16384 | tf_op jit(solution)/shard_map/all_to_all | solution.py:159
  10.0 1.3 slice_bitcast_fusion.9
  11.3 7.7 %collective-permute-start = (bf16[1,8,8,128]{3,2,1,0:T(8,128)(2,1)}, bf16[1,8,8,128]{3,2,1,0:T(8,128)(2,1)S(1)}, u32[]{:S(2)}, u32[]{:S(2)}) collective-permute-start(bf16[1,8,8,128]{3,2,1,0:T(8,128)(2,1)} %slice_bitcast_fusion.9), channel_id=1, source_target_pairs={{1,0},{2,1},{3,2},{4,3},{5,4},{6,5},{7,6},{8,7},{9,8},{10,9},{11,1... | collective-permute-start | bytes 49160 | tf_op jit(solution)/shard_map/ppermute | solution.py:15
  19.0 1.6 slice_bitcast_fusion.4
  20.5 2.8 %collective-permute-start.2 = (bf16[8,8,8,128]{3,2,1,0:T(8,128)(2,1)}, bf16[8,8,8,128]{3,2,1,0:T(8,128)(2,1)}, u32[]{:S(2)}, u32[]{:S(2)}) collective-permute-start(bf16[8,8,8,128]{3,2,1,0:T(8,128)(2,1)} %slice_bitcast_fusion.4), channel_id=1, source_target_pairs={{1,0},{2,1},{3,2},{4,3},{5,4},{6,5},{7,6},{8,7},{9,8},{10,9},{11,1... | collective-permute-start | bytes 393224 | tf_op jit(solution)/shard_map/ppermute | solution.py:15
  23.3 2.0 %fusion.113 = (bf16[8,8,8,1,128]{4,3,2,1,0:T(2,128)(2,1)S(1)}, bf16[8,8,8,1,128]{4,3,2,1,0:T(2,128)(2,1)S(1)}) fusion(bf16[8,8,8,8,128]{4,3,2,1,0:T(8,128)(2,1)} %bitcast.269), kind=kLoop, calls=%fused_computation.195 | loop fusion | bytes 524288 | tf_op jit(solution)/shard_map/slice | solution.py:42
  26.0 2.5 %collective-permute-start.4 = (bf16[8,8,8,128]{3,2,1,0:T(8,128)(2,1)}, bf16[8,8,8,128]{3,2,1,0:T(8,128)(2,1)}, u32[]{:S(2)}, u32[]{:S(2)}) collective-permute-start(bf16[8,8,8,128]{3,2,1,0:T(8,128)(2,1)} %bitcast.266), channel_id=1, source_target_pairs={{1,0},{2,1},{3,2},{4,3},{5,4},{6,5},{7,6},{8,7},{9,8},{10,9},{11,1... | collective-permute-start | bytes 393224 | tf_op jit(solution)/shard_map/ppermute | solution.py:15
  28.5 1.2 compare_and_fusion
  30.4 1.7 fusion.116
  32.1 1.6 fusion.115
  33.7 1.8 fusion.114
  36.1 2.6 %fusion.78 = f32[4096,128]{1,0:T(8,128)} fusion(bf16[4096,128]{1,0:T(8,128)(2,1)S(1)} %bitcast.273, bf16[7,128,128]{2,1,0:T(8,128)(2,1)} %param.15), kind=kOutput, calls=%fused_computation.147 | convolution fusion | flops 134217728 | bytes 3178496 | tf_op jit(solution)/shard_map/dot_general | solution.py:68
  39.3 1.6 reshape.292
  40.9 2.8 %gather_fusion = bf16[8,1024,256]{2,1,0:T(8,128)(2,1)} fusion(bf16[4,1024,256]{2,1,0:T(8,128)(2,1)S(1)} %copy-done, s32[1024]{0:T(1024)S(1)} %pad_clamp_fusion), kind=kCustom, calls=%fused_computation | custom fusion | bytes 8388640 | tf_op jit(solution)/shard_map/jit(_take)/gather | solution.py:143
  43.8 1.4 pad_maximum_fusion.6
  47.3 2.8 %collective-permute-start.1 = (bf16[1,8,8,128]{3,2,1,0:T(8,128)(2,1)S(1)}, bf16[1,8,8,128]{3,2,1,0:T(8,128)(2,1)S(1)}, u32[]{:S(2)}, u32[]{:S(2)}) collective-permute-start(bf16[1,8,8,128]{3,2,1,0:T(8,128)(2,1)S(1)} %slice.408), channel_id=1, source_target_pairs={{0,1},{1,2},{2,3},{3,4},{4,5},{5,6},{6,7},{7,8},{8,9},{9,10},{10,1... | collective-permute-start | bytes 49160 | tf_op jit(solution)/shard_map/ppermute | solution.py:15
  50.2 2.5 %collective-permute-start.3 = (bf16[8,8,8,128]{3,2,1,0:T(8,128)(2,1)S(1)}, bf16[8,8,8,128]{3,2,1,0:T(8,128)(2,1)S(1)}, u32[]{:S(2)}, u32[]{:S(2)}) collective-permute-start(bf16[8,8,8,128]{3,2,1,0:T(8,128)(2,1)S(1)} %get-tuple-element.47), channel_id=1, source_target_pairs={{0,1},{1,2},{2,3},{3,4},{4,5},{5,6},{6,7},{7,8},{8,9},{9,10},{10,1... | collective-permute-start | bytes 393224 | tf_op jit(solution)/shard_map/ppermute | solution.py:15
  53.7 1.9 collective-permute-start.5
  57.0 7.2 %collective-permute-done.5 = bf16[8,8,8,128]{3,2,1,0:T(8,128)(2,1)S(1)} collective-permute-done((bf16[8,8,8,128]{3,2,1,0:T(8,128)(2,1)S(1)}, bf16[8,8,8,128]{3,2,1,0:T(8,128)(2,1)S(1)}, u32[]{:S(2)}, u32[]{:S(2)}) %collective-permute-start.5) | collective-permute-done | bytes 131104 | tf_op jit(solution)/shard_map/ppermute | solution.py:15
  69.3 3.7 %collective-permute-start.6 = (bf16[1,8,8,128]{3,2,1,0:T(8,128)(2,1)S(1)}, bf16[1,8,8,128]{3,2,1,0:T(8,128)(2,1)S(1)}, u32[]{:S(2)}, u32[]{:S(2)}) collective-permute-start(bf16[1,8,8,128]{3,2,1,0:T(8,128)(2,1)S(1)} %slice_bitcast_fusion.8), channel_id=1, source_target_pairs={{1,0},{2,1},{3,2},{4,3},{5,4},{6,5},{7,6},{8,7},{9,8},{10,9},{11,1... | collective-permute-start | bytes 49160 | tf_op jit(solution)/shard_map/ppermute | solution.py:15
  73.0 2.1 %collective-permute-start.8 = (bf16[8,8,8,128]{3,2,1,0:T(8,128)(2,1)S(1)}, bf16[8,8,8,128]{3,2,1,0:T(8,128)(2,1)S(1)}, u32[]{:S(2)}, u32[]{:S(2)}) collective-permute-start(bf16[8,8,8,128]{3,2,1,0:T(8,128)(2,1)S(1)} %slice_bitcast_fusion.1), channel_id=1, source_target_pairs={{1,0},{2,1},{3,2},{4,3},{5,4},{6,5},{7,6},{8,7},{9,8},{10,9},{11,1... | collective-permute-start | bytes 393224 | tf_op jit(solution)/shard_map/ppermute | solution.py:15
  75.1 1.9 collective-permute-start.10
  78.8 3.2 %collective-permute-start.7 = (bf16[1,8,8,128]{3,2,1,0:T(8,128)(2,1)S(1)}, bf16[1,8,8,128]{3,2,1,0:T(8,128)(2,1)S(1)}, u32[]{:S(2)}, u32[]{:S(2)}) collective-permute-start(bf16[1,8,8,128]{3,2,1,0:T(8,128)(2,1)S(1)} %slice.423), channel_id=1, source_target_pairs={{0,1},{1,2},{2,3},{3,4},{4,5},{5,6},{6,7},{7,8},{8,9},{9,10},{10,1... | collective-permute-start | bytes 49160 | tf_op jit(solution)/shard_map/ppermute | solution.py:15
  82.0 3.1 %collective-permute-start.9 = (bf16[8,8,8,128]{3,2,1,0:T(8,128)(2,1)S(1)}, bf16[8,8,8,128]{3,2,1,0:T(8,128)(2,1)S(1)}, u32[]{:S(2)}, u32[]{:S(2)}) collective-permute-start(bf16[8,8,8,128]{3,2,1,0:T(8,128)(2,1)S(1)} %get-tuple-element.37), channel_id=1, source_target_pairs={{0,1},{1,2},{2,3},{3,4},{4,5},{5,6},{6,7},{7,8},{8,9},{9,10},{10,1... | collective-permute-start | bytes 393224 | tf_op jit(solution)/shard_map/ppermute | solution.py:15
  85.2 2.1 %collective-permute-start.11 = (bf16[8,8,8,128]{3,2,1,0:T(8,128)(2,1)S(1)}, bf16[8,8,8,128]{3,2,1,0:T(8,128)(2,1)S(1)}, u32[]{:S(2)}, u32[]{:S(2)}) collective-permute-start(bf16[8,8,8,128]{3,2,1,0:T(8,128)(2,1)S(1)} %get-tuple-element.56), channel_id=1, source_target_pairs={{0,1},{1,2},{2,3},{3,4},{4,5},{5,6},{6,7},{7,8},{8,9},{9,10},{10,1... | collective-permute-start | bytes 393224 | tf_op jit(solution)/shard_map/ppermute | solution.py:15
  89.2 6.0 %collective-permute-done.11 = bf16[8,8,8,128]{3,2,1,0:T(8,128)(2,1)S(1)} collective-permute-done((bf16[8,8,8,128]{3,2,1,0:T(8,128)(2,1)S(1)}, bf16[8,8,8,128]{3,2,1,0:T(8,128)(2,1)S(1)}, u32[]{:S(2)}, u32[]{:S(2)}) %collective-permute-start.11) | collective-permute-done | bytes 131104 | tf_op jit(solution)/shard_map/ppermute | solution.py:15
  97.0 1.7 convolution_add_fusion
  98.7 2.9 %reshape.272 = f32[8,64,1024]{2,1,0:T(8,128)} reshape(f32[4096,128]{1,0:T(8,128)} %convolution_add_fusion) | data formatting | bytes 4194304 | tf_op jit(solution)/shard_map/reshape | solution.py:95
  101.7 3.8 %fusion.2 = f32[8,64,256]{2,1,0:T(8,128)S(1)} fusion(bf16[8,1024,256]{2,1,0:T(8,128)(2,1)} %gather_fusion, pred[8]{0:T(512)(128)(4,1)S(1)} %copy-done.18, f32[8,64,1024]{2,1,0:T(8,128)S(1)} %copy-done.3, f32[8,64,1024]{2,1,0:T(8,128)} %reshape.272), kind=kOutput, calls=%fused_computation.15 | convolution fusion | flops 272105472 | bytes 8912904 | tf_op jit(solution)/shard_map/bpk,bkn->bpn/dot_general | solution.py:144
  106.7 3.0 %copy.218 = f32[16,2,16384]{2,1,0:T(2,128)} copy(f32[16,2,16384]{2,0,1:T(8,128)S(1)} %fusion.98) | data formatting | bytes 4194304 | tf_op jit(solution)/shard_map/dot_general | solution.py:148
  109.6 3.7 %all-to-all-start.1 = ((f32[16,2,16384]{2,1,0:T(2,128)}), f32[16,2,16384]{2,1,0:T(2,128)S(1)}, u32[]{:S(2)}, u32[]{:S(2)}) async-start(f32[16,2,16384]{2,1,0:T(2,128)} %copy.218), calls=%async_computation.1 | async-start | bytes 4194304 | tf_op jit(solution)/shard_map/all_to_all | solution.py:156
  114.7 28.2 %all-to-all-done.1 = f32[16,2,16384]{2,1,0:T(2,128)S(1)} async-done(((f32[16,2,16384]{2,1,0:T(2,128)}), f32[16,2,16384]{2,1,0:T(2,128)S(1)}, u32[]{:S(2)}, u32[]{:S(2)}) %all-to-all-start.1) | async-done | bytes 2097184 | tf_op jit(solution)/shard_map/all_to_all | solution.py:156
  142.8 2.4 %reshape.274 = f32[32,16384]{1,0:T(8,128)} reshape(f32[16,2,16384]{2,1,0:T(2,128)S(1)} %all-to-all-done.1) | data formatting | bytes 4194304 | tf_op jit(solution)/shard_map/reshape | solution.py:161
  145.3 2.2 %copy.232 = f32[4,8,64,256]{3,2,1,0:T(8,128)S(1)} copy(f32[4,8,64,256]{3,1,2,0:T(8,128)} %bitcast.295) | data formatting | bytes 4194304
  147.5 2.5 %fusion.16 = bf16[8,8,4,8,256]{4,0,3,1,2:T(8,128)(2,1)S(1)} fusion(f32[8,8,256,32]{2,1,0,3:T(8,128)S(1)} %bitcast.294, f32[8,4]{0,1:T(4,128)S(1)} %multiply_add_fusion, f32[32]{0:T(128)S(1)} %eq.50), kind=kOutput, calls=%fused_computation.43 | convolution fusion | flops 201851904 | bytes 3145984 | tf_op jit(solution)/shard_map/dot_general | solution.py:166
  150.3 6.5 %collective-permute-start.12 = (bf16[1,32,256]{2,1,0:T(8,128)(2,1)S(1)}, bf16[1,32,256]{2,1,0:T(8,128)(2,1)S(1)}, u32[]{:S(2)}, u32[]{:S(2)}) collective-permute-start(bf16[1,32,256]{2,1,0:T(8,128)(2,1)S(1)} %get-tuple-element.31), channel_id=1, source_target_pairs={{0,16},{16,32},{32,48},{48,64},{64,80},{80,96},{96,112},{1,17},{17... | collective-permute-start | bytes 49160 | tf_op jit(solution)/shard_map/ppermute | solution.py:26
  156.8 2.1 %collective-permute-start.13 = (bf16[1,32,256]{2,1,0:T(8,128)(2,1)S(1)}, bf16[1,32,256]{2,1,0:T(8,128)(2,1)S(1)}, u32[]{:S(2)}, u32[]{:S(2)}) collective-permute-start(bf16[1,32,256]{2,1,0:T(8,128)(2,1)S(1)} %get-tuple-element.32), channel_id=1, source_target_pairs={{16,0},{32,16},{48,32},{64,48},{80,64},{96,80},{112,96},{17,1},{33... | collective-permute-start | bytes 49160 | tf_op jit(solution)/shard_map/ppermute | solution.py:28
  158.9 3.1 %collective-permute-done.13 = bf16[1,32,256]{2,1,0:T(8,128)(2,1)S(1)} collective-permute-done((bf16[1,32,256]{2,1,0:T(8,128)(2,1)S(1)}, bf16[1,32,256]{2,1,0:T(8,128)(2,1)S(1)}, u32[]{:S(2)}, u32[]{:S(2)}) %collective-permute-start.13) | collective-permute-done | bytes 16416 | tf_op jit(solution)/shard_map/ppermute | solution.py:28
  162.1 2.1 %collective-permute-start.14 = (bf16[66,1,256]{2,1,0:T(2,128)(2,1)S(1)}, bf16[66,1,256]{2,1,0:T(2,128)(2,1)S(1)}, u32[]{:S(2)}, u32[]{:S(2)}) collective-permute-start(bf16[66,1,256]{2,1,0:T(2,128)(2,1)S(1)} %get-tuple-element.23), channel_id=1, source_target_pairs={{0,1},{1,2},{2,3},{3,4},{4,5},{5,6},{6,7},{7,8},{8,9},{9,10},{10,1... | collective-permute-start | bytes 101384 | tf_op jit(solution)/shard_map/ppermute | solution.py:26
  164.2 1.5 collective-permute-start.15
  166.4 2.9 %collective-permute-done.15 = bf16[66,1,256]{2,1,0:T(2,128)(2,1)S(1)} collective-permute-done((bf16[66,1,256]{2,1,0:T(2,128)(2,1)S(1)}, bf16[66,1,256]{2,1,0:T(2,128)(2,1)S(1)}, u32[]{:S(2)}, u32[]{:S(2)}) %collective-permute-start.15) | collective-permute-done | bytes 33824 | tf_op jit(solution)/shard_map/ppermute | solution.py:28
  174.9 3.5 %collective-permute-start.16 = (bf16[1,32,256]{2,1,0:T(8,128)(2,1)S(1)}, bf16[1,32,256]{2,1,0:T(8,128)(2,1)S(1)}, u32[]{:S(2)}, u32[]{:S(2)}) collective-permute-start(bf16[1,32,256]{2,1,0:T(8,128)(2,1)S(1)} %get-tuple-element.27), channel_id=1, source_target_pairs={{0,16},{16,32},{32,48},{48,64},{64,80},{80,96},{96,112},{1,17},{17... | collective-permute-start | bytes 49160 | tf_op jit(solution)/shard_map/ppermute | solution.py:26
  178.3 1.9 collective-permute-start.17
  180.3 3.1 %collective-permute-done.17 = bf16[1,32,256]{2,1,0:T(8,128)(2,1)S(1)} collective-permute-done((bf16[1,32,256]{2,1,0:T(8,128)(2,1)S(1)}, bf16[1,32,256]{2,1,0:T(8,128)(2,1)S(1)}, u32[]{:S(2)}, u32[]{:S(2)}) %collective-permute-start.17) | collective-permute-done | bytes 16416 | tf_op jit(solution)/shard_map/ppermute | solution.py:28
  183.5 2.1 %collective-permute-start.18 = (bf16[66,1,256]{2,1,0:T(2,128)(2,1)S(1)}, bf16[66,1,256]{2,1,0:T(2,128)(2,1)S(1)}, u32[]{:S(2)}, u32[]{:S(2)}) collective-permute-start(bf16[66,1,256]{2,1,0:T(2,128)(2,1)S(1)} %get-tuple-element.19), channel_id=1, source_target_pairs={{0,1},{1,2},{2,3},{3,4},{4,5},{5,6},{6,7},{7,8},{8,9},{9,10},{10,1... | collective-permute-start | bytes 101384 | tf_op jit(solution)/shard_map/ppermute | solution.py:26
  185.6 1.3 collective-permute-start.19
  187.5 3.1 %collective-permute-done.19 = bf16[66,1,256]{2,1,0:T(2,128)(2,1)S(1)} collective-permute-done((bf16[66,1,256]{2,1,0:T(2,128)(2,1)S(1)}, bf16[66,1,256]{2,1,0:T(2,128)(2,1)S(1)}, u32[]{:S(2)}, u32[]{:S(2)}) %collective-permute-start.19) | collective-permute-done | bytes 33824 | tf_op jit(solution)/shard_map/ppermute | solution.py:28
  196.3 1.4 add_convert_fusion
  (147 shorter events, 34.6 us)
Async XLA Ops:
  0.0 40.9 %copy-start = (bf16[4,1024,256]{2,1,0:T(8,128)(2,1)S(1)}, bf16[4,1024,256]{2,1,0:T(8,128)(2,1)}, u32[]{:S(2)}) copy-start(bf16[4,1024,256]{2,1,0:T(8,128)(2,1)} %param.17) | copy-start | bytes 6291460
  0.0 30.4 %copy-start.2 = (bf16[8,512,128]{2,1,0:T(8,128)(2,1)S(1)}, bf16[8,512,128]{2,1,0:T(8,128)(2,1)}, u32[]{:S(2)}) copy-start(bf16[8,512,128]{2,1,0:T(8,128)(2,1)} %param.10) | copy-start | bytes 3145732
  1.5 108.1 %all-to-all-start = ((f32[16,1,2]{2,1,0:T(1,128)}), f32[16,1,2]{2,1,0:T(1,128)S(1)}, u32[]{:S(2)}, u32[]{:S(2)}) async-start(f32[16,1,2]{2,1,0:T(1,128)} %bitcast), calls=%async_computation | async-start | bytes 16384 | tf_op jit(solution)/shard_map/all_to_all | solution.py:159
  11.3 32.4 %collective-permute-start = (bf16[1,8,8,128]{3,2,1,0:T(8,128)(2,1)}, bf16[1,8,8,128]{3,2,1,0:T(8,128)(2,1)S(1)}, u32[]{:S(2)}, u32[]{:S(2)}) collective-permute-start(bf16[1,8,8,128]{3,2,1,0:T(8,128)(2,1)} %slice_bitcast_fusion.9), channel_id=1, source_target_pairs={{1,0},{2,1},{3,2},{4,3},{5,4},{6,5},{7,6},{8,7},{9,8},{10,9},{11,1... | collective-permute-start | bytes 49160 | tf_op jit(solution)/shard_map/ppermute | solution.py:15
  20.5 25.5 %collective-permute-start.2 = (bf16[8,8,8,128]{3,2,1,0:T(8,128)(2,1)}, bf16[8,8,8,128]{3,2,1,0:T(8,128)(2,1)}, u32[]{:S(2)}, u32[]{:S(2)}) collective-permute-start(bf16[8,8,8,128]{3,2,1,0:T(8,128)(2,1)} %slice_bitcast_fusion.4), channel_id=1, source_target_pairs={{1,0},{2,1},{3,2},{4,3},{5,4},{6,5},{7,6},{8,7},{9,8},{10,9},{11,1... | collective-permute-start | bytes 393224 | tf_op jit(solution)/shard_map/ppermute | solution.py:15
  26.0 26.7 %collective-permute-start.4 = (bf16[8,8,8,128]{3,2,1,0:T(8,128)(2,1)}, bf16[8,8,8,128]{3,2,1,0:T(8,128)(2,1)}, u32[]{:S(2)}, u32[]{:S(2)}) collective-permute-start(bf16[8,8,8,128]{3,2,1,0:T(8,128)(2,1)} %bitcast.266), channel_id=1, source_target_pairs={{1,0},{2,1},{3,2},{4,3},{5,4},{6,5},{7,6},{8,7},{9,8},{10,9},{11,1... | collective-permute-start | bytes 393224 | tf_op jit(solution)/shard_map/ppermute | solution.py:15
  33.7 1.8 copy-start.16
  43.7 1.9 copy-start.4
  43.7 1.9 copy-start.12
  45.6 0.7 copy-start.14
  45.6 7.1 %copy-start.15 = (bf16[8]{0:T(256)(128)(2,1)S(1)}, bf16[8]{0:T(256)(128)(2,1)}, u32[]{:S(2)}) copy-start(bf16[8]{0:T(256)(128)(2,1)} %get-tuple-element.53) | copy-start | bytes 52
  45.6 10.1 %copy-start.9 = (bf16[8,8,7,8,128]{4,3,2,1,0:T(8,128)(2,1)S(1)}, bf16[8,8,7,8,128]{4,3,2,1,0:T(8,128)(2,1)}, u32[]{:S(2)}) copy-start(bf16[8,8,7,8,128]{4,3,2,1,0:T(8,128)(2,1)} %get-tuple-element.50) | copy-start | bytes 2752516
  46.2 9.8 %copy-start.8 = (bf16[8,7,8,8,128]{4,3,2,1,0:T(8,128)(2,1)S(1)}, bf16[8,7,8,8,128]{4,3,2,1,0:T(8,128)(2,1)}, u32[]{:S(2)}) copy-start(bf16[8,7,8,8,128]{4,3,2,1,0:T(8,128)(2,1)} %get-tuple-element.51) | copy-start | bytes 2752516
  47.3 8.6 %collective-permute-start.1 = (bf16[1,8,8,128]{3,2,1,0:T(8,128)(2,1)S(1)}, bf16[1,8,8,128]{3,2,1,0:T(8,128)(2,1)S(1)}, u32[]{:S(2)}, u32[]{:S(2)}) collective-permute-start(bf16[1,8,8,128]{3,2,1,0:T(8,128)(2,1)S(1)} %slice.408), channel_id=1, source_target_pairs={{0,1},{1,2},{2,3},{3,4},{4,5},{5,6},{6,7},{7,8},{8,9},{9,10},{10,1... | collective-permute-start | bytes 49160 | tf_op jit(solution)/shard_map/ppermute | solution.py:15
  50.2 14.2 %collective-permute-start.3 = (bf16[8,8,8,128]{3,2,1,0:T(8,128)(2,1)S(1)}, bf16[8,8,8,128]{3,2,1,0:T(8,128)(2,1)S(1)}, u32[]{:S(2)}, u32[]{:S(2)}) collective-permute-start(bf16[8,8,8,128]{3,2,1,0:T(8,128)(2,1)S(1)} %get-tuple-element.47), channel_id=1, source_target_pairs={{0,1},{1,2},{2,3},{3,4},{4,5},{5,6},{6,7},{7,8},{8,9},{9,10},{10,1... | collective-permute-start | bytes 393224 | tf_op jit(solution)/shard_map/ppermute | solution.py:15
  53.7 10.5 %collective-permute-start.5 = (bf16[8,8,8,128]{3,2,1,0:T(8,128)(2,1)S(1)}, bf16[8,8,8,128]{3,2,1,0:T(8,128)(2,1)S(1)}, u32[]{:S(2)}, u32[]{:S(2)}) collective-permute-start(bf16[8,8,8,128]{3,2,1,0:T(8,128)(2,1)S(1)} %get-tuple-element.59), channel_id=1, source_target_pairs={{0,1},{1,2},{2,3},{3,4},{4,5},{5,6},{6,7},{7,8},{8,9},{9,10},{10,1... | collective-permute-start | bytes 393224 | tf_op jit(solution)/shard_map/ppermute | solution.py:15
  56.5 7.8 %copy-start.7 = (bf16[8,8,7,8,128]{4,3,2,1,0:T(8,128)(2,1)S(1)}, bf16[8,8,7,8,128]{4,3,2,1,0:T(8,128)(2,1)}, u32[]{:S(2)}) copy-start(bf16[8,8,7,8,128]{4,3,2,1,0:T(8,128)(2,1)} %get-tuple-element.49) | copy-start | bytes 2752516
  64.5 1.2 copy-start.5
  64.5 1.5 copy-start.6
  68.8 8.3 %copy-start.13 = (bf16[7,128,128]{2,1,0:T(8,128)(2,1)S(1)}, bf16[7,128,128]{2,1,0:T(8,128)(2,1)}, u32[]{:S(2)}) copy-start(bf16[7,128,128]{2,1,0:T(8,128)(2,1)} %param.16) | copy-start | bytes 688132
  69.3 8.6 %collective-permute-start.6 = (bf16[1,8,8,128]{3,2,1,0:T(8,128)(2,1)S(1)}, bf16[1,8,8,128]{3,2,1,0:T(8,128)(2,1)S(1)}, u32[]{:S(2)}, u32[]{:S(2)}) collective-permute-start(bf16[1,8,8,128]{3,2,1,0:T(8,128)(2,1)S(1)} %slice_bitcast_fusion.8), channel_id=1, source_target_pairs={{1,0},{2,1},{3,2},{4,3},{5,4},{6,5},{7,6},{8,7},{9,8},{10,9},{11,1... | collective-permute-start | bytes 49160 | tf_op jit(solution)/shard_map/ppermute | solution.py:15
  73.0 5.7 %collective-permute-start.8 = (bf16[8,8,8,128]{3,2,1,0:T(8,128)(2,1)S(1)}, bf16[8,8,8,128]{3,2,1,0:T(8,128)(2,1)S(1)}, u32[]{:S(2)}, u32[]{:S(2)}) collective-permute-start(bf16[8,8,8,128]{3,2,1,0:T(8,128)(2,1)S(1)} %slice_bitcast_fusion.1), channel_id=1, source_target_pairs={{1,0},{2,1},{3,2},{4,3},{5,4},{6,5},{7,6},{8,7},{9,8},{10,9},{11,1... | collective-permute-start | bytes 393224 | tf_op jit(solution)/shard_map/ppermute | solution.py:15
  75.1 10.0 %collective-permute-start.10 = (bf16[8,8,8,128]{3,2,1,0:T(8,128)(2,1)S(1)}, bf16[8,8,8,128]{3,2,1,0:T(8,128)(2,1)S(1)}, u32[]{:S(2)}, u32[]{:S(2)}) collective-permute-start(bf16[8,8,8,128]{3,2,1,0:T(8,128)(2,1)S(1)} %bitcast.326), channel_id=1, source_target_pairs={{1,0},{2,1},{3,2},{4,3},{5,4},{6,5},{7,6},{8,7},{9,8},{10,9},{11,1... | collective-permute-start | bytes 393224 | tf_op jit(solution)/shard_map/ppermute | solution.py:15
  78.8 9.4 %collective-permute-start.7 = (bf16[1,8,8,128]{3,2,1,0:T(8,128)(2,1)S(1)}, bf16[1,8,8,128]{3,2,1,0:T(8,128)(2,1)S(1)}, u32[]{:S(2)}, u32[]{:S(2)}) collective-permute-start(bf16[1,8,8,128]{3,2,1,0:T(8,128)(2,1)S(1)} %slice.423), channel_id=1, source_target_pairs={{0,1},{1,2},{2,3},{3,4},{4,5},{5,6},{6,7},{7,8},{8,9},{9,10},{10,1... | collective-permute-start | bytes 49160 | tf_op jit(solution)/shard_map/ppermute | solution.py:15
  82.0 13.5 %collective-permute-start.9 = (bf16[8,8,8,128]{3,2,1,0:T(8,128)(2,1)S(1)}, bf16[8,8,8,128]{3,2,1,0:T(8,128)(2,1)S(1)}, u32[]{:S(2)}, u32[]{:S(2)}) collective-permute-start(bf16[8,8,8,128]{3,2,1,0:T(8,128)(2,1)S(1)} %get-tuple-element.37), channel_id=1, source_target_pairs={{0,1},{1,2},{2,3},{3,4},{4,5},{5,6},{6,7},{7,8},{8,9},{9,10},{10,1... | collective-permute-start | bytes 393224 | tf_op jit(solution)/shard_map/ppermute | solution.py:15
  85.2 10.0 %collective-permute-start.11 = (bf16[8,8,8,128]{3,2,1,0:T(8,128)(2,1)S(1)}, bf16[8,8,8,128]{3,2,1,0:T(8,128)(2,1)S(1)}, u32[]{:S(2)}, u32[]{:S(2)}) collective-permute-start(bf16[8,8,8,128]{3,2,1,0:T(8,128)(2,1)S(1)} %get-tuple-element.56), channel_id=1, source_target_pairs={{0,1},{1,2},{2,3},{3,4},{4,5},{5,6},{6,7},{7,8},{8,9},{9,10},{10,1... | collective-permute-start | bytes 393224 | tf_op jit(solution)/shard_map/ppermute | solution.py:15
  98.7 2.9 %copy-start.3 = (f32[8,64,1024]{2,1,0:T(8,128)S(1)}, f32[8,64,1024]{2,1,0:T(8,128)}, u32[]{:S(2)}) copy-start(f32[8,64,1024]{2,1,0:T(8,128)} %reshape.292) | copy-start | bytes 6291460
  98.7 2.9 %copy-start.18 = (pred[8]{0:T(512)(128)(4,1)S(1)}, pred[8]{0:T(512)(128)(4,1)}, u32[]{:S(2)}) copy-start(pred[8]{0:T(512)(128)(4,1)} %compare_and_fusion) | copy-start | bytes 28
  101.6 3.9 %copy-start.17 = (s32[16,2]{0,1:T(2,128)S(1)}, s32[16,2]{0,1:T(2,128)}, u32[]{:S(2)}) copy-start(s32[16,2]{0,1:T(2,128)} %multiply_add_fusion.1) | copy-start | bytes 388
  101.7 3.9 %copy-start.19 = (s32[8]{0:T(128)S(1)}, s32[8]{0:T(128)}, u32[]{:S(2)}) copy-start(s32[8]{0:T(128)} %param.12) | copy-start | bytes 100
  109.6 33.2 %all-to-all-start.1 = ((f32[16,2,16384]{2,1,0:T(2,128)}), f32[16,2,16384]{2,1,0:T(2,128)S(1)}, u32[]{:S(2)}, u32[]{:S(2)}) async-start(f32[16,2,16384]{2,1,0:T(2,128)} %copy.218), calls=%async_computation.1 | async-start | bytes 4194304 | tf_op jit(solution)/shard_map/all_to_all | solution.py:156
  150.3 8.6 %collective-permute-start.12 = (bf16[1,32,256]{2,1,0:T(8,128)(2,1)S(1)}, bf16[1,32,256]{2,1,0:T(8,128)(2,1)S(1)}, u32[]{:S(2)}, u32[]{:S(2)}) collective-permute-start(bf16[1,32,256]{2,1,0:T(8,128)(2,1)S(1)} %get-tuple-element.31), channel_id=1, source_target_pairs={{0,16},{16,32},{32,48},{48,64},{64,80},{80,96},{96,112},{1,17},{17... | collective-permute-start | bytes 49160 | tf_op jit(solution)/shard_map/ppermute | solution.py:26
  156.8 9.1 %copy-start.11 = (bf16[3,3,256,256]{3,2,1,0:T(8,128)(2,1)S(1)}, bf16[3,3,256,256]{3,2,1,0:T(8,128)(2,1)}, u32[]{:S(2)}) copy-start(bf16[3,3,256,256]{3,2,1,0:T(8,128)(2,1)} %param.18) | copy-start | bytes 3538948
  156.8 5.2 %collective-permute-start.13 = (bf16[1,32,256]{2,1,0:T(8,128)(2,1)S(1)}, bf16[1,32,256]{2,1,0:T(8,128)(2,1)S(1)}, u32[]{:S(2)}, u32[]{:S(2)}) collective-permute-start(bf16[1,32,256]{2,1,0:T(8,128)(2,1)S(1)} %get-tuple-element.32), channel_id=1, source_target_pairs={{16,0},{32,16},{48,32},{64,48},{80,64},{96,80},{112,96},{17,1},{33... | collective-permute-start | bytes 49160 | tf_op jit(solution)/shard_map/ppermute | solution.py:28
  162.1 4.3 %collective-permute-start.14 = (bf16[66,1,256]{2,1,0:T(2,128)(2,1)S(1)}, bf16[66,1,256]{2,1,0:T(2,128)(2,1)S(1)}, u32[]{:S(2)}, u32[]{:S(2)}) collective-permute-start(bf16[66,1,256]{2,1,0:T(2,128)(2,1)S(1)} %get-tuple-element.23), channel_id=1, source_target_pairs={{0,1},{1,2},{2,3},{3,4},{4,5},{5,6},{6,7},{7,8},{8,9},{9,10},{10,1... | collective-permute-start | bytes 101384 | tf_op jit(solution)/shard_map/ppermute | solution.py:26
  164.2 5.0 %collective-permute-start.15 = (bf16[66,1,256]{2,1,0:T(2,128)(2,1)S(1)}, bf16[66,1,256]{2,1,0:T(2,128)(2,1)S(1)}, u32[]{:S(2)}, u32[]{:S(2)}) collective-permute-start(bf16[66,1,256]{2,1,0:T(2,128)(2,1)S(1)} %get-tuple-element.24), channel_id=1, source_target_pairs={{1,0},{2,1},{3,2},{4,3},{5,4},{6,5},{7,6},{8,7},{9,8},{10,9},{11,1... | collective-permute-start | bytes 101384 | tf_op jit(solution)/shard_map/ppermute | solution.py:28
  174.9 5.4 %collective-permute-start.16 = (bf16[1,32,256]{2,1,0:T(8,128)(2,1)S(1)}, bf16[1,32,256]{2,1,0:T(8,128)(2,1)S(1)}, u32[]{:S(2)}, u32[]{:S(2)}) collective-permute-start(bf16[1,32,256]{2,1,0:T(8,128)(2,1)S(1)} %get-tuple-element.27), channel_id=1, source_target_pairs={{0,16},{16,32},{32,48},{48,64},{64,80},{80,96},{96,112},{1,17},{17... | collective-permute-start | bytes 49160 | tf_op jit(solution)/shard_map/ppermute | solution.py:26
  178.3 5.1 %collective-permute-start.17 = (bf16[1,32,256]{2,1,0:T(8,128)(2,1)S(1)}, bf16[1,32,256]{2,1,0:T(8,128)(2,1)S(1)}, u32[]{:S(2)}, u32[]{:S(2)}) collective-permute-start(bf16[1,32,256]{2,1,0:T(8,128)(2,1)S(1)} %get-tuple-element.28), channel_id=1, source_target_pairs={{16,0},{32,16},{48,32},{64,48},{80,64},{96,80},{112,96},{17,1},{33... | collective-permute-start | bytes 49160 | tf_op jit(solution)/shard_map/ppermute | solution.py:28
  183.4 3.6 %copy-start.10 = (bf16[3,3,256,256]{3,2,1,0:T(8,128)(2,1)S(1)}, bf16[3,3,256,256]{3,2,1,0:T(8,128)(2,1)}, u32[]{:S(2)}) copy-start(bf16[3,3,256,256]{3,2,1,0:T(8,128)(2,1)} %param.19) | copy-start | bytes 3538948
  183.5 4.0 %collective-permute-start.18 = (bf16[66,1,256]{2,1,0:T(2,128)(2,1)S(1)}, bf16[66,1,256]{2,1,0:T(2,128)(2,1)S(1)}, u32[]{:S(2)}, u32[]{:S(2)}) collective-permute-start(bf16[66,1,256]{2,1,0:T(2,128)(2,1)S(1)} %get-tuple-element.19), channel_id=1, source_target_pairs={{0,1},{1,2},{2,3},{3,4},{4,5},{5,6},{6,7},{7,8},{8,9},{9,10},{10,1... | collective-permute-start | bytes 101384 | tf_op jit(solution)/shard_map/ppermute | solution.py:26
  185.6 5.0 %collective-permute-start.19 = (bf16[66,1,256]{2,1,0:T(2,128)(2,1)S(1)}, bf16[66,1,256]{2,1,0:T(2,128)(2,1)S(1)}, u32[]{:S(2)}, u32[]{:S(2)}) collective-permute-start(bf16[66,1,256]{2,1,0:T(2,128)(2,1)S(1)} %get-tuple-element.20), channel_id=1, source_target_pairs={{1,0},{2,1},{3,2},{4,3},{5,4},{6,5},{7,6},{8,7},{9,8},{10,9},{11,1... | collective-permute-start | bytes 101384 | tf_op jit(solution)/shard_map/ppermute | solution.py:28
  196.3 2.0 copy-start.1
where the time goes:
time: 200 us; the launch traced here: 198 us
  starting transfers between devices  69.4 us (35%)
  waiting for transfers between devices  53.9 us (27%)
  local copies, waits for them, and re-layouts  34.8 us (17%)
  matrix products  24.7 us (12%)
  other arithmetic  14.5 us (7%)
    ppermute x12, starting transfers between devices, from_behind(): return lax.ppermute(block, axis, route)  36.3 us
    all_to_all x1, waiting for transfers between devices, local(): lax.all_to_all(summed.reshape(peer_count, per_peer, -1), 'gx', split_axis...  28.2 us
    ppermute x4, starting transfers between devices, padded_2(): lax.ppermute(tail, axis, [(i, (i + 1) % count) for i in range(ends)])  14.2 us
    ppermute x12, waiting for transfers between devices, from_behind(): return lax.ppermute(block, axis, route)  13.5 us
    ppermute x4, waiting for transfers between devices, padded_2(): lax.ppermute(head, axis, [((i + 1) % count, i) for i in range(ends)])  12.3 us
    all_to_all x1, starting transfers between devices, local(): lax.all_to_all(column_ids, 'gx', split_axis=0, concat_axis=0, tiled=True)  8.43 us
    dot_general x18, matrix products, plane_conv(): jnp.dot(window, kernel[row_off, col_off], preferred_element_type=jnp.floa...  8.09 us
    ppermute x4, starting transfers between devices, padded_2(): lax.ppermute(head, axis, [((i + 1) % count, i) for i in range(ends)])  6.78 us
  transfers between devices with their start and end apart: 22, of which 8 were waited for; matrix products, arithmetic and copies ran while one was open for 25% of the time, Pallas kernels for 0%

commit v1 on v0

v1 whole, which is shorter than its diff:
```python
import jax
import jax.numpy as jnp
from jax import lax
from jax.experimental import pallas as pl
from jax.experimental.pallas import tpu as pltpu
from jax.sharding import PartitionSpec as P

NY = 8
NX = 16
MESH = pl.DeviceIdType.MESH
F32 = jnp.float32
BF = jnp.bfloat16


def iota(shape, dim):
    return lax.broadcasted_iota(jnp.int32, shape, dim)


def shr(x, n):
    return lax.shift_right_logical(x, jnp.int32(n))


def onehot(cond):
    return jnp.where(cond, 1.0, 0.0).astype(BF)


def mm(a, b):
    return jnp.dot(a, b, preferred_element_type=F32)


def kernel(
    x_hbm, links, slot, level, ids_in, w1_hbm, w2_hbm, h_hbm, p1_hbm, p2_hbm,
    out,
    xv, w1, w2, hw, p1, p2,
    fa, fb, stage, ghost, astage, aghost,
    perm, up1, dn1, pick, spread,
    sbuf, rbuf, ids, idl,
    bev, first, cstage, cland, rstage, rland, kland,
    wsem, hsend, hrecv, asend, arecv, tsend, trecv, isend, irecv, msend, mrecv,
):
    gy = lax.axis_index("gy")
    gx = lax.axis_index("gx")
    nxt = ((gy + (gx + 1) // NX) % NY, (gx + 1) % NX)
    prv = ((gy + NY - 1 + (gx + NX - 1) // NX) % NY, (gx + NX - 1) % NX)
    north, south = (gy + NY - 1) % NY, (gy + 1) % NY
    west, east = (gx + NX - 1) % NX, (gx + 1) % NX

    loads = [
        pltpu.make_async_copy(s, d, wsem.at[n])
        for n, (s, d) in enumerate(
            [(x_hbm, xv), (w1_hbm, w1), (w2_hbm, w2), (h_hbm, hw), (p1_hbm, p1), (p2_hbm, p2)]
        )
    ]
    for load in loads:
        load.start()

    barrier = pltpu.get_barrier_semaphore()

    def hello(where):
        pl.semaphore_signal(barrier, inc=1, device_id=where, device_id_type=MESH)

    hello(nxt)
    hello(prv)
    for v in (north, gy, south):
        for h in (west, gx, east):
            if v is gy and h is gx:
                continue
            hello((v, h))

    def greet(o, carry):
        hello((gy, (gx + o) % NX))
        return carry

    lax.fori_loop(1, NX, greet, 0)

    r = iota((256, 256), 0)
    q = iota((256, 256), 1)
    perm[...] = onehot(q == (r & 15) * 16 + shr(r, 4))
    up1[...] = onehot((q == r + 1) & ((r & 15) != 15))
    dn1[...] = onehot((q == r - 1) & ((r & 15) != 0))
    r = iota((16, 256), 0)
    q = iota((16, 256), 1)
    pick[0] = onehot(q == r * 16)
    pick[1] = onehot(q == r * 16 + 15)
    r = iota((256, 16), 0)
    q = iota((256, 16), 1)
    spread[0] = onehot(r == q * 16)
    spread[1] = onehot(r == q * 16 + 15)

    ids[...] = jnp.zeros((8, 128), F32)
    ids[0:1, 0:32] = ids_in[...].astype(F32)

    s16 = iota((16, 128), 0)

    def per_block(read, index):
        m = jnp.zeros((16, 128), F32)
        for i in range(8):
            m = jnp.where(index == i, read(i).astype(F32), m)
        return m

    m1 = per_block(lambda i: links[i, 1], shr(s16, 1))
    m2 = per_block(lambda i: links[i, 2], shr(s16, 1))
    ma = jnp.where((s16 & 1) == 0, 1.0, per_block(lambda i: links[i, 0], shr(s16, 1)))
    mb = jnp.where((s16 & 1) == 1, 1.0, per_block(lambda i: links[i, 0], shr(s16, 1) - 1))
    not_last = jnp.where((gx < NX - 1) | (gy < NY - 1), 1.0, 0.0).astype(F32)
    not_first = jnp.where((gx > 0) | (gy > 0), 1.0, 0.0).astype(F32)
    m1p = m1 * not_last
    m2p = m2 * not_last
    top = links[7, 0].astype(F32)

    def times(x, m):
        return (x.astype(F32) * m).astype(BF)

    def face_copy(ph, way, al):
        return pltpu.make_async_remote_copy(
            src_ref=stage.at[ph, way, al],
            dst_ref=ghost.at[ph, way, al],
            send_sem=hsend.at[ph, way, al],
            recv_sem=hrecv.at[ph, way, al],
            device_id=nxt if way else prv,
            device_id_type=MESH,
        )

    def end_copy(ph, way):
        return pltpu.make_async_remote_copy(
            src_ref=astage.at[ph, way],
            dst_ref=aghost.at[ph, way],
            send_sem=asend.at[ph, way],
            recv_sem=arecv.at[ph, way],
            device_id=nxt if way else prv,
            device_id_type=MESH,
        )

    def publish(ph, arr, al):
        stage[ph, 0, al, 0] = arr[al + 1, 1, 1:9]
        stage[ph, 0, al, 1] = arr[al + 1, 1:9, 1]
        stage[ph, 1, al, 0] = times(arr[al + 1, 8, 1:9], m1)
        stage[ph, 1, al, 1] = times(arr[al + 1, 1:9, 8], m2)
        face_copy(ph, 0, al).start()
        face_copy(ph, 1, al).start()

    def publish_end(ph, arr, way):
        for g in range(4):
            rows = arr[4 if way else 1, 1 + 2 * g : 3 + 2 * g, 1:9].reshape(256, 128)
            face = mm(pick[way], rows)
            if way:
                face = face * top
            astage[ph, way, g * 16 : g * 16 + 16] = face.astype(BF)
        end_copy(ph, way).start()

    def absorb(ph, arr, al):
        face_copy(ph, 0, al).wait_recv()
        face_copy(ph, 1, al).wait_recv()
        arr[al + 1, 9, 1:9] = times(ghost[ph, 0, al, 0], m1p)
        arr[al + 1, 1:9, 9] = times(ghost[ph, 0, al, 1], m2p)
        arr[al + 1, 0, 1:9] = times(ghost[ph, 1, al, 0], not_first)
        arr[al + 1, 1:9, 0] = times(ghost[ph, 1, al, 1], not_first)

    def absorb_ends(ph, arr):
        end_copy(ph, 0).wait_recv()
        end_copy(ph, 1).wait_recv()
        for g in range(4):
            bs = slice(1 + 2 * g, 3 + 2 * g)
            gs = slice(g * 16, g * 16 + 16)
            rows = mm(up1[...], arr[1, bs, 1:9].reshape(256, 128)).reshape(16, 16, 128) * ma
            end = mm(spread[1], aghost[ph, 0, gs]).reshape(16, 16, 128) * (top * not_last)
            arr[5, bs, 1:9] = (rows + end).astype(BF).reshape(2, 8, 16, 128)
            rows = mm(dn1[...], arr[4, bs, 1:9].reshape(256, 128)).reshape(16, 16, 128) * mb
            end = mm(spread[0], aghost[ph, 1, gs]).reshape(16, 16, 128) * not_first
            arr[0, bs, 1:9] = (rows + end).astype(BF).reshape(2, 8, 16, 128)

    def taps(arr, al, b0, nb):
        n = nb * 128
        win = [
            arr[al + 1, 1 + b0 : 1 + b0 + nb, 1:9],
            arr[al + 2, 1 + b0 : 1 + b0 + nb, 1:9],
            arr[al, 1 + b0 : 1 + b0 + nb, 1:9],
            arr[al + 1, 2 + b0 : 2 + b0 + nb, 1:9],
            arr[al + 1, b0 : b0 + nb, 1:9],
            arr[al + 1, 1 + b0 : 1 + b0 + nb, 2:10],
            arr[al + 1, 1 + b0 : 1 + b0 + nb, 0:8],
        ]
        return jnp.concatenate([w.reshape(n, 128) for w in win], axis=1)

    loads[0].wait()
    pl.semaphore_wait(barrier, 25)

    def send_ids(o, carry):
        pltpu.make_async_remote_copy(
            src_ref=ids,
            dst_ref=idl.at[gx],
            send_sem=isend,
            recv_sem=irecv,
            device_id=(gy, (gx + o) % NX),
            device_id_type=MESH,
        ).start()
        return carry

    def bring(t, carry):
        al = (t + 3) % 4
        for g in (0, 2):
            two = [
                xv[:, :, al, k * 16 : k * 16 + 16, :].reshape(256, 128) for k in (g, g + 1)
            ]
            moved = mm(perm[...], jnp.concatenate(two, axis=1)).astype(BF)
            for n in range(2):
                fa[al + 1, 1 + 2 * (g + n) : 3 + 2 * (g + n), 1:9] = moved[
                    :, n * 128 : n * 128 + 128
                ].reshape(2, 8, 16, 128)
        publish(0, fa, al)
        return carry

    lax.fori_loop(0, 4, bring, 0)
    publish_end(0, fa, 0)
    publish_end(0, fa, 1)
    lax.fori_loop(1, NX, send_ids, 0)
    idl[gx] = ids[...]

    loads[1].wait()
    absorb_ends(0, fa)

    def conv_one(t, carry):
        al = (t + 3) % 4
        absorb(0, fa, al)
        for b0 in (0, 4):
            h = mm(taps(fa, al, b0, 4), w1[...])
            fb[al + 1, 1 + b0 : 5 + b0, 1:9] = (
                jnp.maximum(h, 0.0).astype(BF).reshape(4, 8, 16, 128)
            )
        publish(1, fb, al)

        @pl.when(t == 0)
        def _():
            publish_end(1, fb, 1)

        @pl.when(t == 1)
        def _():
            publish_end(1, fb, 0)

        return carry

    lax.fori_loop(0, 4, conv_one, 0)

    lane = iota((1, 128), 1)
    slot_lane = jnp.zeros((1, 128), jnp.int32)
    for i in range(8):
        slot_lane = jnp.where((shr(lane, 1) & 7) == i, slot[i], slot_lane)
    k = iota((512, 128), 0)
    rho = iota((512, 128), 1)
    slot_mat = onehot(
        (shr(k, 4) == slot_lane) & ((shr(k, 1) & 7) == shr(rho, 4)) & ((k & 1) == (rho & 1))
    )
    row_block = shr(iota((128, 256), 0), 1) & 7
    row_level = jnp.zeros((128, 256), jnp.int32)
    for i in range(8):
        row_level = jnp.where(row_block == i, level[i], row_level)

    loads[2].wait()
    loads[3].wait()
    absorb_ends(1, fb)

    def column_copy(al, o):
        to = (gx + o) % NX
        return pltpu.make_async_remote_copy(
            src_ref=sbuf.at[al, to],
            dst_ref=rbuf.at[al, gx],
            send_sem=tsend.at[al],
            recv_sem=trecv.at[al],
            device_id=(gy, to),
            device_id_type=MESH,
        )

    def conv_two(t, carry):
        al = (t + 3) % 4
        absorb(1, fb, al)
        parts = []
        for b0 in (0, 4):
            v = mm(taps(fb, al, b0, 4), w2[...])
            v = v + fa[al + 1, 1 + b0 : 5 + b0, 1:9].reshape(512, 128).astype(F32)
            v = jnp.maximum(v, 0.0).astype(BF).reshape(4, 8, 16, 128)
            parts.append(
                jnp.concatenate([v[:, c].reshape(64, 128) for c in range(8)], axis=1)
            )
        rows = jnp.concatenate(parts, axis=0)
        lifted = jnp.zeros((128, 256), F32)
        for lv in range(4):
            lifted = jnp.where(row_level == lv, mm(rows, hw[lv]), lifted)
        high = lifted.astype(BF)
        low = (lifted - high.astype(F32)).astype(BF)
        sums = mm(slot_mat, high) + mm(slot_mat, low)
        sbuf[al] = sums.astype(BF).reshape(16, 32, 256)

        def send(o, c):
            column_copy(al, o).start()
            return c

        lax.fori_loop(1, NX, send, 0)
        rbuf[al, gx] = sbuf[al, gx]
        return carry

    lax.fori_loop(0, 4, conv_two, 0)

    pltpu.make_async_copy(idl.at[0:15], idl.at[0:15], irecv).wait()
    sel = onehot(iota((128, 512), 0) == 2 * gx + (shr(iota((128, 512), 1), 4) & 1))
    got = mm(idl[...].reshape(128, 128).astype(BF), sel)
    rr = iota((128, 512), 0)
    kk = iota((128, 512), 1)
    got = jnp.where(((rr & 7) == 0) & (shr(rr, 3) == shr(kk, 5)), got, 0.0)
    cid = jnp.sum(got, axis=0, keepdims=True)
    r = iota((512, 512), 0)
    k = iota((512, 512), 1)
    want = (shr(r, 1) & 7) * 4 + shr(r, 7)
    tile_mat = onehot(
        (cid == want.astype(F32)) & ((shr(r, 4) & 7) == (shr(k, 1) & 7)) & ((r & 1) == (k & 1))
    )

    def gather(t, carry):
        al = (t + 3) % 4
        pltpu.make_async_copy(rbuf.at[al, 0:15], rbuf.at[al, 0:15], trecv.at[al]).wait()
        tile = mm(tile_mat, rbuf[al].reshape(512, 256))
        bev[al + 2, 2:34] = tile.astype(BF).reshape(32, 16, 256)
        return carry

    lax.fori_loop(0, 4, gather, 0)

    cstage[0] = bev[2:6, 2:4]
    cstage[1] = bev[2:6, 32:34]
    for n in range(2):
        for g in range(2):
            xs = slice(2 + 16 * g, 18 + 16 * g)
            gs = slice(16 * g, 16 * g + 16)
            rstage[0, n, gs] = mm(pick[0], bev[2 + n, xs].reshape(256, 256)).astype(BF)
            rstage[1, n, gs] = mm(pick[1], bev[4 + n, xs].reshape(256, 256)).astype(BF)

    def rim(n, src, dst, where):
        return pltpu.make_async_remote_copy(
            src_ref=src,
            dst_ref=dst,
            send_sem=msend.at[n],
            recv_sem=mrecv.at[n],
            device_id=where,
            device_id_type=MESH,
        )

    rims = [
        rim(0, cstage.at[0], cland.at[0], (gy, west)),
        rim(1, cstage.at[1], cland.at[1], (gy, east)),
        rim(2, rstage.at[0], rland.at[0], (north, gx)),
        rim(3, rstage.at[1], rland.at[1], (south, gx)),
        rim(4, rstage.at[0, :, 0:16], kland.at[0], (north, west)),
        rim(5, rstage.at[0, :, 16:32], kland.at[1], (north, east)),
        rim(6, rstage.at[1, :, 0:16], kland.at[2], (south, west)),
        rim(7, rstage.at[1, :, 16:32], kland.at[3], (south, east)),
    ]
    for c in rims:
        c.start()
    has_n = jnp.where(gy > 0, 1.0, 0.0).astype(F32)
    has_s = jnp.where(gy < NY - 1, 1.0, 0.0).astype(F32)
    has_w = jnp.where(gx > 0, 1.0, 0.0).astype(F32)
    has_e = jnp.where(gx < NX - 1, 1.0, 0.0).astype(F32)
    for c in rims:
        c.wait_recv()
    bev[2:6, 34:36] = times(cland[0], has_e)
    bev[2:6, 0:2] = times(cland[1], has_w)
    r = iota((32, 16), 0)
    q = iota((32, 16), 1)
    at_start = [onehot((r == q * 16 + 15)), onehot((r == q * 16))]
    at_end = [onehot((r == (q - 14) * 16 + 15)), onehot((r == (q - 14) * 16))]
    for n in range(2):
        for way, src, dst, sh, there in ((0, 2 + n, 6 + n, up1, has_s), (1, 4 + n, n, dn1, has_n)):
            for g in range(2):
                xs = slice(2 + 16 * g, 18 + 16 * g)
                gs = slice(16 * g, 16 * g + 16)
                rows = mm(sh[...], bev[src, xs].reshape(256, 256))
                rows = rows + mm(spread[1 - way], rland[way, n, gs]) * there
                bev[dst, xs] = rows.astype(BF).reshape(16, 16, 256)
            rows = mm(sh[0:32, 0:32], bev[src, 0:2].reshape(32, 256))
            rows = rows + mm(at_end[way], kland[2 * way + 1, n]) * (there * has_w)
            bev[dst, 0:2] = rows.astype(BF).reshape(2, 16, 256)
            rows = mm(sh[0:32, 0:32], bev[src, 34:36].reshape(32, 256))
            rows = rows + mm(at_start[way], kland[2 * way, n]) * (there * has_e)
            bev[dst, 34:36] = rows.astype(BF).reshape(2, 16, 256)
    upper = iota((36, 16, 256), 1) < 8
    for n in range(3):
        bev[8 + n] = jnp.where(upper, bev[n].astype(F32), bev[5 + n].astype(F32)).astype(BF)

    loads[4].wait()

    def plane_one(t, carry):
        yl = t + 3 * (t // 4)
        win = [
            bev[yl + 1 + dy, dx : dx + 34].reshape(544, 256)
            for dy in range(3)
            for dx in range(3)
        ]
        f = mm(jnp.concatenate(win, axis=1), p1[...])
        first[t + 1, 0:34] = jnp.maximum(f, 0.0).astype(BF).reshape(34, 16, 256)
        return carry

    lax.fori_loop(0, 5, plane_one, 0)
    first[1:6, 0:1] = times(first[1:6, 0:1], has_w)
    first[1:6, 33:34] = times(first[1:6, 33:34], has_e)
    for x0, n in ((0, 16), (16, 16), (32, 2)):
        m = n * 16
        xs = slice(x0, x0 + n)
        edge = first[5, xs].reshape(m, 256).astype(F32)
        row = iota((m, 256), 0) & 15
        below = mm(up1[0:m, 0:m], first[1, xs].reshape(m, 256))
        below = jnp.where(row == 15, edge * has_s, below)
        above = mm(dn1[0:m, 0:m], first[4, xs].reshape(m, 256))
        above = jnp.where(row == 0, edge * has_n, above)
        first[0, xs] = above.astype(BF).reshape(n, 16, 256)
        first[5, xs] = below.astype(BF).reshape(n, 16, 256)

    loads[5].wait()

    def plane_two(yl, carry):
        win = [
            first[yl + dy, dx : dx + 32].reshape(512, 256) for dy in range(3) for dx in range(3)
        ]
        s = mm(jnp.concatenate(win, axis=1), p2[...])
        s = (s + bev[yl + 2, 2:34].reshape(512, 256).astype(F32)).astype(BF)
        for g in range(2):
            moved = mm(perm[...], s[256 * g : 256 * g + 256]).astype(BF)
            out[:, yl, 16 * g : 16 * g + 16, :] = moved.reshape(16, 16, 256)
        return carry

    lax.fori_loop(0, 4, plane_two, 0)

    for ph in range(2):
        for way in range(2):
            end_copy(ph, way).wait_send()
            for al in range(4):
                face_copy(ph, way, al).wait_send()
    for al in range(4):
        pltpu.make_async_copy(sbuf.at[al, 0:15], sbuf.at[al, 0:15], tsend.at[al]).wait()
    pltpu.make_async_copy(idl.at[0:15], idl.at[0:15], isend).wait()
    for c in rims:
        c.wait_send()


def local(
    features, links, block_slot, block_level, slot_column,
    conv_first, conv_second, height_w, plane_first, plane_second,
):
    hbm = pl.BlockSpec(memory_space=pl.ANY)
    smem = pl.BlockSpec(memory_space=pltpu.SMEM)
    vmem = pl.BlockSpec(memory_space=pltpu.VMEM)
    dma = pltpu.SemaphoreType.DMA
    out = pl.pallas_call(
        kernel,
        out_shape=jax.ShapeDtypeStruct((16, 4, 32, 256), BF),
        in_specs=[hbm, smem, smem, smem, vmem, hbm, hbm, hbm, hbm, hbm],
        out_specs=vmem,
        scratch_shapes=[
            pltpu.VMEM((8, 2, 4, 64, 128), BF),
            pltpu.VMEM((896, 128), BF),
            pltpu.VMEM((896, 128), BF),
            pltpu.VMEM((4, 1024, 256), BF),
            pltpu.VMEM((2304, 256), BF),
            pltpu.VMEM((2304, 256), BF),
            pltpu.VMEM((6, 10, 10, 16, 128), BF),
            pltpu.VMEM((6, 10, 10, 16, 128), BF),
            pltpu.VMEM((2, 2, 4, 2, 8, 16, 128), BF),
            pltpu.VMEM((2, 2, 4, 2, 8, 16, 128), BF),
            pltpu.VMEM((2, 2, 64, 128), BF),
            pltpu.VMEM((2, 2, 64, 128), BF),
            pltpu.VMEM((256, 256), BF),
            pltpu.VMEM((256, 256), BF),
            pltpu.VMEM((256, 256), BF),
            pltpu.VMEM((2, 16, 256), BF),
            pltpu.VMEM((2, 256, 16), BF),
            pltpu.VMEM((4, 16, 32, 256), BF),
            pltpu.VMEM((4, 16, 32, 256), BF),
            pltpu.VMEM((8, 128), F32),
            pltpu.VMEM((16, 8, 128), F32),
            pltpu.VMEM((11, 36, 16, 256), BF),
            pltpu.VMEM((6, 34, 16, 256), BF),
            pltpu.VMEM((2, 4, 2, 16, 256), BF),
            pltpu.VMEM((2, 4, 2, 16, 256), BF),
            pltpu.VMEM((2, 2, 32, 256), BF),
            pltpu.VMEM((2, 2, 32, 256), BF),
            pltpu.VMEM((4, 2, 16, 256), BF),
            dma((6,)),
            dma((2, 2, 4)),
            dma((2, 2, 4)),
            dma((2, 2)),
            dma((2, 2)),
            dma((4,)),
            dma((4,)),
            dma,
            dma,
            dma((8,)),
            dma((8,)),
        ],
        compiler_params=pltpu.CompilerParams(
            collective_id=0, has_side_effects=True, vmem_limit_bytes=56 * 2**20
        ),
    )(
        features.reshape(8, 2, 4, 64, 128),
        links,
        block_slot,
        block_level,
        slot_column,
        conv_first.reshape(896, 128),
        conv_second.reshape(896, 128),
        height_w,
        plane_first.reshape(2304, 256),
        plane_second.reshape(2304, 256),
    )
    return out.reshape(64, 32, 256)


def solution(mesh):
    in_specs = (
        P(("gy", "gx"), None, None),
        P(("gy", "gx"), None),
        P(("gy", "gx")),
        P(("gy", "gx")),
        P(("gy", "gx"), None),
        P(),
        P(),
        P(),
        P(),
        P(),
    )
    return jax.shard_map(
        local, mesh=mesh, in_specs=in_specs, out_specs=P("gy", "gx", None), check_vma=False
    )
```

time: 200 us -> 63.6 us (0.32)
  starting transfers between devices: 69.4 us -> 0 us
  Pallas kernels: 0 us -> 59.8 us
  waiting for transfers between devices: 53.9 us -> 0 us
  local copies, waits for them, and re-layouts: 34.8 us -> 3.61 us
  matrix products: 24.7 us -> 0 us
  other arithmetic: 14.5 us -> 0 us
    pallas_call x0 -> x1, Pallas kernels: none -> 59.8 us  [local(): pl.pallas_call(kernel, out_shape=jax.ShapeDtypeStruct((16, 4, 32, 256), B...]
    ppermute x20 -> x0, starting transfers between devices: 57.3 us -> none  [the longest x12 36.3 us: from_behind(): return lax.ppermute(block, axis, route)]
    all_to_all x2 -> x0, waiting for transfers between devices: 28.2 us -> none  [the longest x1 28.2 us: local(): lax.all_to_all(summed.reshape(peer_count, per_peer, -1), 'gx', split_axis...]
    ppermute x20 -> x0, waiting for transfers between devices: 25.7 us -> none  [the longest x12 13.5 us: from_behind(): return lax.ppermute(block, axis, route)]
    dot_general x35 -> x0, matrix products: 24.7 us -> none  [the longest x18 8.09 us: plane_conv(): jnp.dot(window, kernel[row_off, col_off], preferred_element_type=jnp.floa...]
    slice x22 -> x0, local copies, waits for them, and re-layouts: 12.2 us -> none  [the longest x6 6.22 us: seven_taps(): lax.slice_in_dim(blocks, 0, EDGE - 1, axis=axis)]
    all_to_all x2 -> x0, starting transfers between devices: 12.1 us -> none  [the longest x1 8.43 us: local(): lax.all_to_all(column_ids, 'gx', split_axis=0, concat_axis=0, tiled=True)]
    concatenate x15 -> x0, other arithmetic: 6.34 us -> none  [the longest x6 3.36 us: seven_taps(): jnp.concatenate([lax.slice_in_dim(blocks, 1, EDGE, axis=axis), jnp.expand...]
  transfers between devices with their start and end apart: 22 -> 0, of which waited for: 8 -> 0; matrix products, arithmetic and copies ran while one was open for 25% -> 0% of each run, Pallas kernels for 0% -> 0%
where the time goes in v1:
time: 63.6 us; the launch traced here: 63.4 us
  Pallas kernels  59.8 us (94%)
  local copies, waits for them, and re-layouts  3.61 us (6%)
    pallas_call x1, Pallas kernels, local(): pl.pallas_call(kernel, out_shape=jax.ShapeDtypeStruct((16, 4, 32, 256), B...  59.8 us
    unnamed x2, local copies, waits for them, and re-layouts  3.61 us

profile of v1, /device:TPU:1, one launch (start us, length us, event | category | flops | bytes accessed | tf_op | source)
XLA Modules:
  0.0 63.4 jit_solution(9642087062568382028)
XLA Ops:
  0.0 1.3 %copy.11.links = s32[8,3]{1,0:T(8,128)} copy(s32[8,3]{0,1:T(4,128)} %param.11) | data formatting | bytes 192 | tf_op args[1]
  1.3 59.8 %shard_map.100 = bf16[16,4,32,256]{3,2,1,0:T(8,128)(2,1)} custom-call(bf16[8,2,4,64,128]{4,3,2,1,0:T(8,128)(2,1)} %bitcast.9, s32[8,3]{1,0:T(8,128)} %copy.11.links, s32[8]{0:T(128)} %slot.1, s32[8]{0:T(128)} %level.1, s32[1,32]{1,0:T(1,128)} %ids_in.1, bf16[896,128]{1,0:T(8,128)(2,1)} %bitcast.10, bf16[896,128]{1,0:T(8,128)(2,1)} %bitcast.11, ...), custom_call_target="tpu_custom_call" | custom-call | tf_op jit(solution)/shard_map/pallas_call | solution.py:450
  61.1 2.3 %copy.13 = bf16[64,32,256]{2,1,0:T(8,128)(2,1)} copy(bf16[64,32,256]{2,1,0:T(8,128)(2,1)} %bitcast.6) | data formatting | bytes 2097152

commit v2 on v1

--- a/solution.py
+++ b/solution.py
@@ -29,13 +29,13 @@
 
 
 def kernel(
-    x_hbm, links, slot, level, ids_in, w1_hbm, w2_hbm, h_hbm, p1_hbm, p2_hbm,
-    out,
-    xv, w1, w2, hw, p1, p2,
+    x_hbm, links_hbm, slot_hbm, level_hbm, ids_hbm, w1_hbm, w2_hbm, h_hbm, p1_hbm,
+    first, base,
+    links, slot, level, ids_in, xv, w1, w2, hw, p1,
     fa, fb, stage, ghost, astage, aghost,
     perm, up1, dn1, pick, spread,
     sbuf, rbuf, ids, idl,
-    bev, first, cstage, cland, rstage, rland, kland,
+    bev, edge, cstage, cland, rstage, rland, kland,
     wsem, hsend, hrecv, asend, arecv, tsend, trecv, isend, irecv, msend, mrecv,
 ):
     gy = lax.axis_index("gy")
@@ -48,7 +48,10 @@
     loads = [
         pltpu.make_async_copy(s, d, wsem.at[n])
         for n, (s, d) in enumerate(
-            [(x_hbm, xv), (w1_hbm, w1), (w2_hbm, w2), (h_hbm, hw), (p1_hbm, p1), (p2_hbm, p2)]
+            [
+                (x_hbm, xv), (w1_hbm, w1), (w2_hbm, w2), (h_hbm, hw), (p1_hbm, p1),
+                (links_hbm, links), (slot_hbm, slot), (level_hbm, level), (ids_hbm, ids_in),
+            ]
         )
     ]
     for load in loads:
@@ -87,7 +90,9 @@
     spread[0] = onehot(r == q * 16)
     spread[1] = onehot(r == q * 16 + 15)
 
-    ids[...] = jnp.zeros((8, 128), F32)
+    for load in loads[5:]:
+        load.wait()
+    ids[...] = jnp.zeros((1, 128), F32)
     ids[0:1, 0:32] = ids_in[...].astype(F32)
 
     s16 = iota((16, 128), 0)
@@ -98,15 +103,15 @@
             m = jnp.where(index == i, read(i).astype(F32), m)
         return m
 
-    m1 = per_block(lambda i: links[i, 1], shr(s16, 1))
-    m2 = per_block(lambda i: links[i, 2], shr(s16, 1))
-    ma = jnp.where((s16 & 1) == 0, 1.0, per_block(lambda i: links[i, 0], shr(s16, 1)))
-    mb = jnp.where((s16 & 1) == 1, 1.0, per_block(lambda i: links[i, 0], shr(s16, 1) - 1))
+    m1 = per_block(lambda i: links[1, i], shr(s16, 1))
+    m2 = per_block(lambda i: links[2, i], shr(s16, 1))
+    ma = jnp.where((s16 & 1) == 0, 1.0, per_block(lambda i: links[0, i], shr(s16, 1)))
+    mb = jnp.where((s16 & 1) == 1, 1.0, per_block(lambda i: links[0, i], shr(s16, 1) - 1))
     not_last = jnp.where((gx < NX - 1) | (gy < NY - 1), 1.0, 0.0).astype(F32)
     not_first = jnp.where((gx > 0) | (gy > 0), 1.0, 0.0).astype(F32)
     m1p = m1 * not_last
     m2p = m2 * not_last
-    top = links[7, 0].astype(F32)
+    top = links[0, 7].astype(F32)
 
     def times(x, m):
         return (x.astype(F32) * m).astype(BF)
@@ -210,10 +215,11 @@
         publish(0, fa, al)
         return carry
 
+    astage[0, 0] = xv[0, 0, 0]
+    astage[0, 1] = (xv[7, 1, 3].astype(F32) * top).astype(BF)
+    end_copy(0, 0).start()
+    end_copy(0, 1).start()
     lax.fori_loop(0, 4, bring, 0)
-    publish_end(0, fa, 0)
-    publish_end(0, fa, 1)
-    lax.fori_loop(1, NX, send_ids, 0)
     idl[gx] = ids[...]
 
     loads[1].wait()
@@ -240,6 +246,7 @@
         return carry
 
     lax.fori_loop(0, 4, conv_one, 0)
+    lax.fori_loop(1, NX, send_ids, 0)
 
     lane = iota((1, 128), 1)
     slot_lane = jnp.zeros((1, 128), jnp.int32)
@@ -302,10 +309,8 @@
 
     pltpu.make_async_copy(idl.at[0:15], idl.at[0:15], irecv).wait()
     sel = onehot(iota((128, 512), 0) == 2 * gx + (shr(iota((128, 512), 1), 4) & 1))
-    got = mm(idl[...].reshape(128, 128).astype(BF), sel)
-    rr = iota((128, 512), 0)
-    kk = iota((128, 512), 1)
-    got = jnp.where(((rr & 7) == 0) & (shr(rr, 3) == shr(kk, 5)), got, 0.0)
+    got = mm(idl[...].reshape(16, 128).astype(BF), sel)
+    got = jnp.where(iota((16, 512), 0) == shr(iota((16, 512), 1), 5), got, 0.0)
     cid = jnp.sum(got, axis=0, keepdims=True)
     r = iota((512, 512), 0)
     k = iota((512, 512), 1)
@@ -358,74 +363,106 @@
     has_s = jnp.where(gy < NY - 1, 1.0, 0.0).astype(F32)
     has_w = jnp.where(gx > 0, 1.0, 0.0).astype(F32)
     has_e = jnp.where(gx < NX - 1, 1.0, 0.0).astype(F32)
+
+    def carry_over(mat, arr, dst, src, x0, n):
+        rows = mm(mat[0 : 16 * n, 0 : 16 * n], arr[src, x0 : x0 + n].reshape(16 * n, 256))
+        arr[dst, x0 : x0 + n] = rows.astype(BF).reshape(n, 16, 256)
+
+    for x0 in (2, 18):
+        carry_over(dn1, bev, 1, 5, x0, 16)
+        carry_over(up1, bev, 6, 2, x0, 16)
+
+    loads[4].wait()
+
+    def plane_inner(yl, carry):
+        win = [
+            bev[yl + 1 + dy, 2 + dx : 32 + dx].reshape(480, 256)
+            for dy in range(3)
+            for dx in range(3)
+        ]
+        f = mm(jnp.concatenate(win, axis=1), p1[...])
+        first[yl + 1, 2:32] = jnp.maximum(f, 0.0).astype(BF).reshape(30, 16, 256)
+        return carry
+
+    lax.fori_loop(0, 4, plane_inner, 0)
+    for x0, n in ((2, 16), (18, 14)):
+        carry_over(dn1, first, 0, 4, x0, n)
+        carry_over(up1, first, 5, 1, x0, n)
+
     for c in rims:
         c.wait_recv()
     bev[2:6, 34:36] = times(cland[0], has_e)
     bev[2:6, 0:2] = times(cland[1], has_w)
+    for x0 in (0, 34):
+        carry_over(dn1, bev, 1, 5, x0, 2)
+        carry_over(up1, bev, 6, 2, x0, 2)
     r = iota((32, 16), 0)
     q = iota((32, 16), 1)
-    at_start = [onehot((r == q * 16 + 15)), onehot((r == q * 16))]
-    at_end = [onehot((r == (q - 14) * 16 + 15)), onehot((r == (q - 14) * 16))]
+    left_n, left_s = onehot(r == (q - 14) * 16), onehot(r == (q - 14) * 16 + 15)
+    right_n, right_s = onehot(r == q * 16), onehot(r == q * 16 + 15)
     for n in range(2):
-        for way, src, dst, sh, there in ((0, 2 + n, 6 + n, up1, has_s), (1, 4 + n, n, dn1, has_n)):
-            for g in range(2):
-                xs = slice(2 + 16 * g, 18 + 16 * g)
-                gs = slice(16 * g, 16 * g + 16)
-                rows = mm(sh[...], bev[src, xs].reshape(256, 256))
-                rows = rows + mm(spread[1 - way], rland[way, n, gs]) * there
-                bev[dst, xs] = rows.astype(BF).reshape(16, 16, 256)
-            rows = mm(sh[0:32, 0:32], bev[src, 0:2].reshape(32, 256))
-            rows = rows + mm(at_end[way], kland[2 * way + 1, n]) * (there * has_w)
-            bev[dst, 0:2] = rows.astype(BF).reshape(2, 16, 256)
-            rows = mm(sh[0:32, 0:32], bev[src, 34:36].reshape(32, 256))
-            rows = rows + mm(at_start[way], kland[2 * way, n]) * (there * has_e)
-            bev[dst, 34:36] = rows.astype(BF).reshape(2, 16, 256)
-    upper = iota((36, 16, 256), 1) < 8
-    for n in range(3):
-        bev[8 + n] = jnp.where(upper, bev[n].astype(F32), bev[5 + n].astype(F32)).astype(BF)
-
-    loads[4].wait()
-
-    def plane_one(t, carry):
-        yl = t + 3 * (t // 4)
-        win = [
-            bev[yl + 1 + dy, dx : dx + 34].reshape(544, 256)
-            for dy in range(3)
-            for dx in range(3)
-        ]
-        f = mm(jnp.concatenate(win, axis=1), p1[...])
-        first[t + 1, 0:34] = jnp.maximum(f, 0.0).astype(BF).reshape(34, 16, 256)
-        return carry
-
-    lax.fori_loop(0, 5, plane_one, 0)
-    first[1:6, 0:1] = times(first[1:6, 0:1], has_w)
-    first[1:6, 33:34] = times(first[1:6, 33:34], has_e)
-    for x0, n in ((0, 16), (16, 16), (32, 2)):
-        m = n * 16
-        xs = slice(x0, x0 + n)
-        edge = first[5, xs].reshape(m, 256).astype(F32)
-        row = iota((m, 256), 0) & 15
-        below = mm(up1[0:m, 0:m], first[1, xs].reshape(m, 256))
-        below = jnp.where(row == 15, edge * has_s, below)
-        above = mm(dn1[0:m, 0:m], first[4, xs].reshape(m, 256))
-        above = jnp.where(row == 0, edge * has_n, above)
-        first[0, xs] = above.astype(BF).reshape(n, 16, 256)
-        first[5, xs] = below.astype(BF).reshape(n, 16, 256)
-
-    loads[5].wait()
-
-    def plane_two(yl, carry):
-        win = [
-            first[yl + dy, dx : dx + 32].reshape(512, 256) for dy in range(3) for dx in range(3)
-        ]
-        s = mm(jnp.concatenate(win, axis=1), p2[...])
-        s = (s + bev[yl + 2, 2:34].reshape(512, 256).astype(F32)).astype(BF)
+        at = 7 * n
         for g in range(2):
-            moved = mm(perm[...], s[256 * g : 256 * g + 256]).astype(BF)
-            out[:, yl, 16 * g : 16 * g + 16, :] = moved.reshape(16, 16, 256)
-        return carry
-
-    lax.fori_loop(0, 4, plane_two, 0)
+            xs = slice(2 + 16 * g, 18 + 16 * g)
+            gs = slice(16 * g, 16 * g + 16)
+            rows = mm(spread[0], rland[1, n, gs]) * has_n + mm(spread[1], rland[0, n, gs]) * has_s
+            bev[at, xs] = rows.astype(BF).reshape(16, 16, 256)
+        rows = mm(left_n, kland[3, n]) * (has_n * has_w) + mm(left_s, kland[1, n]) * (has_s * has_w)
+        bev[at, 0:2] = rows.astype(BF).reshape(2, 16, 256)
+        rows = mm(right_n, kland[2, n]) * (has_n * has_e) + mm(right_s, kland[0, n]) * (has_s * has_e)
+        bev[at, 34:36] = rows.astype(BF).reshape(2, 16, 256)
+
+    s8 = iota((36, 8, 256), 1)
+    for dy in range(3):
+        top0, top1 = ((0, 7), (7, 2), (2, 3))[dy]
+        low0, low1 = ((4, 5), (5, 0), (0, 7))[dy]
+        here = bev[top0][:, 0:8].astype(F32)
+        after = pltpu.roll(bev[top1][:, 0:8].astype(F32), 1, 1)
+        upper = jnp.where(s8 == 0, here, jnp.where(s8 == 1, after, 0.0))
+        here = bev[low1][:, 8:16].astype(F32)
+        before = pltpu.roll(bev[low0][:, 8:16].astype(F32), 7, 1)
+        lower = jnp.where(s8 == 7, here, jnp.where(s8 == 6, before, 0.0))
+        bev[8 + dy] = jnp.concatenate([upper, lower], axis=1).astype(BF)
+    win = [bev[8 + dy, dx : dx + 34].reshape(544, 256) for dy in range(3) for dx in range(3)]
+    f = mm(jnp.concatenate(win, axis=1), p1[...])
+    edge[...] = jnp.maximum(f, 0.0).reshape(34, 16, 256)
+    win = [
+        jnp.concatenate(
+            [
+                bev[1 + dy : 5 + dy, x0 + dx : x0 + dx + 2].reshape(128, 256) for x0 in (0, 32)
+            ],
+            axis=0,
+        )
+        for dy in range(3)
+        for dx in range(3)
+    ]
+    f = mm(jnp.concatenate(win, axis=1), p1[...])
+    f = jnp.maximum(f, 0.0).reshape(2, 4, 2, 16, 256)
+    first[1:5, 0:1] = (f[0, :, 0:1] * has_w).astype(BF)
+    first[1:5, 1:2] = f[0, :, 1:2].astype(BF)
+    first[1:5, 32:33] = f[1, :, 0:1].astype(BF)
+    first[1:5, 33:34] = (f[1, :, 1:2] * has_e).astype(BF)
+    edge[0:1] = edge[0:1] * has_w
+    edge[33:34] = edge[33:34] * has_e
+    for x0 in (0, 32):
+        carry_over(dn1, first, 0, 4, x0, 2)
+        carry_over(up1, first, 5, 1, x0, 2)
+    s8 = iota((34, 8, 256), 1)
+    upper = edge[:, 0:8]
+    lower = edge[:, 8:16]
+
+    def patch(slab, half, row, new):
+        old = first[slab]
+        keep = old[:, 0:8].astype(F32), old[:, 8:16].astype(F32)
+        mixed = jnp.where(s8 == row, new, keep[half])
+        both = [mixed, keep[1]] if half == 0 else [keep[0], mixed]
+        first[slab] = jnp.concatenate(both, axis=1).astype(BF)
+
+    patch(0, 0, 0, upper * has_n)
+    patch(1, 0, 0, pltpu.roll(upper, 7, 1))
+    patch(4, 1, 7, pltpu.roll(lower, 1, 1))
+    patch(5, 1, 7, lower * has_s)
+    base[...] = bev[2:6, 2:34]
 
     for ph in range(2):
         for way in range(2):
@@ -439,25 +476,62 @@
         c.wait_send()
 
 
+def last_kernel(first, base, p2, out, buf, sems):
+    r = iota((256, 256), 0)
+    q = iota((256, 256), 1)
+    perm = onehot(q == (r & 15) * 16 + shr(r, 4))
+    copies = []
+    for yl in range(4):
+        win = [
+            first[yl + dy, dx : dx + 32].reshape(512, 256) for dy in range(3) for dx in range(3)
+        ]
+        s = mm(jnp.concatenate(win, axis=1), p2[...])
+        s = (s + base[yl].reshape(512, 256).astype(F32)).astype(BF)
+        for g in range(2):
+            moved = mm(perm, s[256 * g : 256 * g + 256]).astype(BF)
+            buf[yl, :, 16 * g : 16 * g + 16, :] = moved.reshape(16, 16, 256)
+        c = pltpu.make_async_copy(buf.at[yl], out.at[:, yl], sems.at[yl])
+        c.start()
+        copies.append(c)
+    for c in copies:
+        c.wait()
+
+
 def local(
     features, links, block_slot, block_level, slot_column,
     conv_first, conv_second, height_w, plane_first, plane_second,
 ):
-    hbm = pl.BlockSpec(memory_space=pl.ANY)
-    smem = pl.BlockSpec(memory_space=pltpu.SMEM)
+    hbm = pl.BlockSpec(memory_space=pltpu.HBM)
     vmem = pl.BlockSpec(memory_space=pltpu.VMEM)
     dma = pltpu.SemaphoreType.DMA
-    out = pl.pallas_call(
+    operands = (
+        features.reshape(8, 2, 4, 64, 128),
+        links.T,
+        block_slot,
+        block_level,
+        slot_column,
+        conv_first.reshape(896, 128),
+        conv_second.reshape(896, 128),
+        height_w,
+        plane_first.reshape(2304, 256),
+    )
+    first, base = pl.pallas_call(
         kernel,
-        out_shape=jax.ShapeDtypeStruct((16, 4, 32, 256), BF),
-        in_specs=[hbm, smem, smem, smem, vmem, hbm, hbm, hbm, hbm, hbm],
-        out_specs=vmem,
+        out_shape=[
+            jax.ShapeDtypeStruct((6, 34, 16, 256), BF),
+            jax.ShapeDtypeStruct((4, 32, 16, 256), BF),
+        ],
+        in_specs=[hbm] * 9,
+        out_specs=[vmem, vmem],
         scratch_shapes=[
+            pltpu.SMEM((3, 8), jnp.int32),
+            pltpu.SMEM((8,), jnp.int32),
+            pltpu.SMEM((8,), jnp.int32),
+            pltpu.VMEM((1, 32), jnp.int32),
             pltpu.VMEM((8, 2, 4, 64, 128), BF),
             pltpu.VMEM((896, 128), BF),
             pltpu.VMEM((896, 128), BF),
             pltpu.VMEM((4, 1024, 256), BF),
-            pltpu.VMEM((2304, 256), BF),
             pltpu.VMEM((2304, 256), BF),
             pltpu.VMEM((6, 10, 10, 16, 128), BF),
             pltpu.VMEM((6, 10, 10, 16, 128), BF),
@@ -472,16 +546,16 @@
             pltpu.VMEM((2, 256, 16), BF),
             pltpu.VMEM((4, 16, 32, 256), BF),
             pltpu.VMEM((4, 16, 32, 256), BF),
-            pltpu.VMEM((8, 128), F32),
-            pltpu.VMEM((16, 8, 128), F32),
+            pltpu.VMEM((1, 128), F32),
+            pltpu.VMEM((16, 1, 128), F32),
             pltpu.VMEM((11, 36, 16, 256), BF),
-            pltpu.VMEM((6, 34, 16, 256), BF),
+            pltpu.VMEM((34, 16, 256), F32),
             pltpu.VMEM((2, 4, 2, 16, 256), BF),
             pltpu.VMEM((2, 4, 2, 16, 256), BF),
             pltpu.VMEM((2, 2, 32, 256), BF),
             pltpu.VMEM((2, 2, 32, 256), BF),
             pltpu.VMEM((4, 2, 16, 256), BF),
-            dma((6,)),
+            dma((9,)),
             dma((2, 2, 4)),
             dma((2, 2, 4)),
             dma((2, 2)),
@@ -494,20 +568,19 @@
             dma((8,)),
         ],
         compiler_params=pltpu.CompilerParams(
-            collective_id=0, has_side_effects=True, vmem_limit_bytes=56 * 2**20
+            collective_id=0, has_side_effects=True, vmem_limit_bytes=40 * 2**20
         ),
     )(
-        features.reshape(8, 2, 4, 64, 128),
-        links,
-        block_slot,
-        block_level,
-        slot_column,
-        conv_first.reshape(896, 128),
-        conv_second.reshape(896, 128),
-        height_w,
-        plane_first.reshape(2304, 256),
-        plane_second.reshape(2304, 256),
+        *[pltpu.with_memory_space_constraint(x, pltpu.HBM) for x in operands]
     )
+    out = pl.pallas_call(
+        last_kernel,
+        out_shape=jax.ShapeDtypeStruct((16, 4, 32, 256), BF),
+        in_specs=[vmem, vmem, vmem],
+        out_specs=hbm,
+        scratch_shapes=[pltpu.VMEM((4, 16, 32, 256), BF), dma((4,))],
+        compiler_params=pltpu.CompilerParams(vmem_limit_bytes=24 * 2**20),
+    )(first, base, plane_second.reshape(2304, 256))
     return out.reshape(64, 32, 256)
 
 

time: 63.6 us -> 51.9 us (0.82)
  Pallas kernels: 59.8 us -> 51.8 us
  local copies, waits for them, and re-layouts: 3.61 us -> 0.01 us
    pallas_call x1 -> x2, Pallas kernels: 59.8 us -> 51.8 us  [the longest x1 45.3 us: local(): pl.pallas_call(kernel, out_shape=[jax.ShapeDtypeStruct((6, 34, 16, 256),...]
    unnamed x2, local copies, waits for them, and re-layouts: 3.61 us -> 0.01 us
where the time goes in v2:
time: 51.9 us; the launch traced here: 51.8 us
  Pallas kernels  51.8 us (100%)
    pallas_call x1, Pallas kernels, local(): pl.pallas_call(kernel, out_shape=[jax.ShapeDtypeStruct((6, 34, 16, 256),...  45.3 us
    pallas_call x1, Pallas kernels, local(): pl.pallas_call(last_kernel, out_shape=jax.ShapeDtypeStruct((16, 4, 32, 25...  6.49 us

profile of v2, /device:TPU:1, one launch (start us, length us, event | category | flops | bytes accessed | tf_op | source)
XLA Modules:
  0.0 51.8 jit_solution(6320122393011996947)
XLA Ops:
  0.0 0.0 copy-start
  0.0 45.3 %shard_map.100 = (bf16[6,34,16,256]{3,2,1,0:T(8,128)(2,1)S(1)}, bf16[4,32,16,256]{3,2,1,0:T(8,128)(2,1)S(1)}) custom-call(bf16[8,2,4,64,128]{4,3,2,1,0:T(8,128)(2,1)} %bitcast.9, s32[3,8]{1,0:T(4,128)} %bitcast.12, s32[8]{0:T(128)} %slot_hbm.1, s32[8]{0:T(128)} %level_hbm.1, s32[1,32]{1,0:T(1,128)} %ids_hbm.1, bf16[896,128]{1,0:T(8,128)(2,1)} %bitcast.10, ...), custom_call_target="tpu_custom_call" | custom-call | tf_op jit(solution)/shard_map/pallas_call | solution.py:518
  45.3 0.0 copy-done
  45.3 6.5 %shard_map.101 = bf16[16,4,32,256]{3,2,1,0:T(8,128)(2,1)} custom-call(bf16[6,34,16,256]{3,2,1,0:T(8,128)(2,1)S(1)} %get-tuple-element.7.first, bf16[4,32,16,256]{3,2,1,0:T(8,128)(2,1)S(1)} %get-tuple-element.8.base, bf16[2304,256]{1,0:T(8,128)(2,1)S(1)} %bitcast.7), custom_call_target="tpu_custom_call" | custom-call | tf_op jit(solution)/shard_map/pallas_call | solution.py:576
Async XLA Ops:
  0.0 45.3 %copy-start = (bf16[3,3,256,256]{3,2,1,0:T(8,128)(2,1)S(1)}, bf16[3,3,256,256]{3,2,1,0:T(8,128)(2,1)}, u32[]{:S(2)}) copy-start(bf16[3,3,256,256]{3,2,1,0:T(8,128)(2,1)} %param.19) | copy-start | bytes 3538948

commit v3 on v2

v3 whole, which is shorter than its diff:
```python
import jax
import jax.numpy as jnp
from jax import lax
from jax.experimental import pallas as pl
from jax.experimental.pallas import tpu as pltpu
from jax.sharding import PartitionSpec as P

NY = 8
NX = 16
MESH = pl.DeviceIdType.MESH
F32 = jnp.float32
BF = jnp.bfloat16


def iota(shape, dim):
    return lax.broadcasted_iota(jnp.int32, shape, dim)


def shr(x, n):
    return lax.shift_right_logical(x, jnp.int32(n))


def onehot(cond):
    return jnp.where(cond, 1.0, 0.0).astype(BF)


def mm(a, b):
    return jnp.dot(a, b, preferred_element_type=F32)


def halves(x):
    x = x.astype(F32)
    return x[:, 0:8], x[:, 8:16]


def one_up(x, last, scale=(1.0, 1.0)):
    low, high = (pltpu.roll(h, 7, 1) for h in halves(x))
    end = iota(low.shape, 1) == 7
    low = jnp.where(end, high, low) * scale[0]
    high = jnp.where(end, last, high * scale[1])
    return jnp.concatenate([low, high], axis=1).astype(BF)


def one_down(x, head, scale=(1.0, 1.0)):
    low, high = (pltpu.roll(h, 1, 1) for h in halves(x))
    end = iota(low.shape, 1) == 0
    high = jnp.where(end, low, high) * scale[1]
    low = jnp.where(end, head, low * scale[0])
    return jnp.concatenate([low, high], axis=1).astype(BF)


def kernel(
    x_hbm, links_hbm, slot_hbm, level_hbm, ids_hbm, w1_hbm, w2_hbm, h_hbm, p1_hbm,
    first, base,
    links, slot, level, ids_in, xv, w1, w2, hw, p1,
    fa, fb, stage, ghost, astage, aghost,
    rows32, sbuf, rbuf, ids, idl,
    bev, edge, tile32, rim32, cstage, cland, rstage, rland, kland,
    wsem, hsend, hrecv, asend, arecv, tsend, trecv, isend, irecv, msend, mrecv,
):
    gy = lax.axis_index("gy")
    gx = lax.axis_index("gx")
    nxt = ((gy + (gx + 1) // NX) % NY, (gx + 1) % NX)
    prv = ((gy + NY - 1 + (gx + NX - 1) // NX) % NY, (gx + NX - 1) % NX)
    north, south = (gy + NY - 1) % NY, (gy + 1) % NY
    west, east = (gx + NX - 1) % NX, (gx + 1) % NX

    loads = [
        pltpu.make_async_copy(s, d, wsem.at[n])
        for n, (s, d) in enumerate(
            [
                (x_hbm, xv), (w1_hbm, w1), (w2_hbm, w2), (h_hbm, hw), (p1_hbm, p1),
                (links_hbm, links), (slot_hbm, slot), (level_hbm, level), (ids_hbm, ids_in),
            ]
        )
    ]
    for load in loads:
        load.start()

    barrier = pltpu.get_barrier_semaphore()

    def hello(where):
        pl.semaphore_signal(barrier, inc=1, device_id=where, device_id_type=MESH)

    has_nxt = (gx < NX - 1) | (gy < NY - 1)
    has_prv = (gx > 0) | (gy > 0)
    can_n, can_s, can_w, can_e = gy > 0, gy < NY - 1, gx > 0, gx < NX - 1
    no = jnp.logical_not

    def greet(o, carry):
        hello((gy, (gx + o) % NX))
        return carry

    greeted = jnp.int32(NX - 1)
    for there, where in (
        (has_nxt, nxt),
        (has_prv, prv),
        (can_n, (north, gx)),
        (can_s, (south, gx)),
        (can_n & can_w, (north, west)),
        (can_n & can_e, (north, east)),
        (can_s & can_w, (south, west)),
        (can_s & can_e, (south, east)),
    ):
        greeted = greeted + there.astype(jnp.int32)

        @pl.when(there)
        def _(where=where):
            hello(where)

    lax.fori_loop(1, NX, greet, 0)

    for there, land in (
        (has_nxt, (ghost.at[:, 0], aghost.at[:, 0])),
        (has_prv, (ghost.at[:, 1], aghost.at[:, 1])),
        (can_e, (cland.at[0],)),
        (can_w, (cland.at[1],)),
        (can_s, (rland.at[0],)),
        (can_n, (rland.at[1],)),
        (can_s & can_e, (kland.at[0],)),
        (can_s & can_w, (kland.at[1],)),
        (can_n & can_e, (kland.at[2],)),
        (can_n & can_w, (kland.at[3],)),
    ):

        @pl.when(no(there))
        def _(land=land):
            for ref in land:
                ref[...] = jnp.zeros(ref.shape, BF)

    for load in loads[5:]:
        load.wait()
    ids[...] = jnp.zeros((1, 128), F32)
    ids[0:1, 0:32] = ids_in[...].astype(F32)

    s16 = iota((16, 128), 0)

    def per_block(read, index):
        m = jnp.zeros((16, 128), F32)
        for i in range(8):
            m = jnp.where(index == i, read(i).astype(F32), m)
        return m

    m1 = per_block(lambda i: links[1, i], shr(s16, 1))
    m2 = per_block(lambda i: links[2, i], shr(s16, 1))
    ma = jnp.where((s16 & 1) == 0, 1.0, per_block(lambda i: links[0, i], shr(s16, 1)))
    mb = jnp.where((s16 & 1) == 1, 1.0, per_block(lambda i: links[0, i], shr(s16, 1) - 1))
    top = links[0, 7].astype(F32)

    def times(x, m):
        return (x.astype(F32) * m).astype(BF)

    def face_copy(ph, way, al):
        return pltpu.make_async_remote_copy(
            src_ref=stage.at[ph, way, al],
            dst_ref=ghost.at[ph, way, al],
            send_sem=hsend.at[ph, way, al],
            recv_sem=hrecv.at[ph, way, al],
            device_id=nxt if way else prv,
            device_id_type=MESH,
        )

    def end_copy(ph, way):
        return pltpu.make_async_remote_copy(
            src_ref=astage.at[ph, way],
            dst_ref=aghost.at[ph, way],
            send_sem=asend.at[ph, way],
            recv_sem=arecv.at[ph, way],
            device_id=nxt if way else prv,
            device_id_type=MESH,
        )

    def ring(do, way, back=False):
        pl.when(has_nxt if (way == 1) != back else has_prv)(do)

    def send_faces(ph, al):
        for way in range(2):
            ring(lambda way=way: face_copy(ph, way, al).start(), way)

    def faces_sent(ph, al):
        for way in range(2):
            ring(lambda way=way: face_copy(ph, way, al).wait_send(), way)

    def lay_out(ph, arr, al):
        stage[ph, 0, al, 0] = arr[al + 1, 1, 1:9]
        stage[ph, 0, al, 1] = arr[al + 1, 1:9, 1]
        stage[ph, 1, al, 0] = times(arr[al + 1, 8, 1:9], m1)
        stage[ph, 1, al, 1] = times(arr[al + 1, 1:9, 8], m2)

    def send_end(ph, way):
        ring(lambda: end_copy(ph, way).start(), way)

    def absorb(ph, arr, al):
        for way in range(2):
            ring(lambda way=way: face_copy(ph, way, al).wait_recv(), way, True)
        arr[al + 1, 9, 1:9] = times(ghost[ph, 0, al, 0], m1)
        arr[al + 1, 1:9, 9] = times(ghost[ph, 0, al, 1], m2)
        arr[al + 1, 0, 1:9] = ghost[ph, 1, al, 0]
        arr[al + 1, 1:9, 0] = ghost[ph, 1, al, 1]

    def absorb_ends(ph, arr):
        for way in range(2):
            ring(lambda way=way: end_copy(ph, way).wait_recv(), way, True)
        rows32[0, pl.ds(15, 64, stride=16), :] = aghost[ph, 0].astype(F32) * top
        rows32[0, pl.ds(0, 64, stride=16), :] = aghost[ph, 1].astype(F32)
        for b in range(8):
            low, high = halves(rows32[0, b * 128 : b * 128 + 128].reshape(8, 16, 128))
            arr[5, 1 + b, 1:9] = one_up(arr[1, 1 + b, 1:9], high, (ma[0:8], ma[8:16]))
            arr[0, 1 + b, 1:9] = one_down(arr[4, 1 + b, 1:9], low, (mb[0:8], mb[8:16]))

    def taps(arr, al, b0, nb):
        n = nb * 128
        win = [
            arr[al + 1, 1 + b0 : 1 + b0 + nb, 1:9],
            arr[al + 2, 1 + b0 : 1 + b0 + nb, 1:9],
            arr[al, 1 + b0 : 1 + b0 + nb, 1:9],
            arr[al + 1, 2 + b0 : 2 + b0 + nb, 1:9],
            arr[al + 1, b0 : b0 + nb, 1:9],
            arr[al + 1, 1 + b0 : 1 + b0 + nb, 2:10],
            arr[al + 1, 1 + b0 : 1 + b0 + nb, 0:8],
        ]
        return jnp.concatenate([w.reshape(n, 128) for w in win], axis=1)

    loads[0].wait()

    def send_ids(o, carry):
        pltpu.make_async_remote_copy(
            src_ref=ids,
            dst_ref=idl.at[gx],
            send_sem=isend,
            recv_sem=irecv,
            device_id=(gy, (gx + o) % NX),
            device_id_type=MESH,
        ).start()
        return carry

    astage[0, 0] = xv[0, 0, 0]
    astage[0, 1] = (xv[7, 1, 3].astype(F32) * top).astype(BF)
    for t in range(4):
        al = (t + 3) % 4
        rows32[t % 2] = xv[:, :, al].reshape(1024, 128).astype(F32)
        for b in range(8):
            for c in range(8):
                cell = rows32[t % 2, pl.ds(8 * b + c, 16, stride=64), :]
                fa[al + 1, 1 + b, 1 + c] = cell.astype(BF)
        lay_out(0, fa, al)
    idl[gx] = ids[...]
    pl.semaphore_wait(barrier, greeted)
    send_end(0, 0)
    send_end(0, 1)
    send_faces(0, 3)
    send_faces(0, 0)
    faces_sent(0, 3)
    send_faces(0, 1)
    faces_sent(0, 0)
    send_faces(0, 2)

    loads[1].wait()
    absorb_ends(0, fa)

    for t in range(4):
        al = (t + 3) % 4
        absorb(0, fa, al)
        for b0 in (0, 4):
            h = jnp.maximum(mm(taps(fa, al, b0, 4), w1[...]), 0.0)
            fb[al + 1, 1 + b0 : 5 + b0, 1:9] = h.astype(BF).reshape(4, 8, 16, 128)
            if t < 2:
                rows32[t, b0 * 128 : b0 * 128 + 512] = h
        if t == 0:
            astage[1, 1] = (rows32[0, pl.ds(15, 64, stride=16), :] * top).astype(BF)
            send_end(1, 1)
        if t == 1:
            astage[1, 0] = rows32[1, pl.ds(0, 64, stride=16), :].astype(BF)
            send_end(1, 0)
        lay_out(1, fb, al)
        send_faces(1, al)

    lax.fori_loop(1, NX, send_ids, 0)

    lane = iota((1, 128), 1)
    slot_lane = jnp.zeros((1, 128), jnp.int32)
    for i in range(8):
        slot_lane = jnp.where((shr(lane, 1) & 7) == i, slot[i], slot_lane)
    slot_lane = jnp.concatenate([slot_lane, slot_lane], axis=1)
    k = iota((512, 256), 0)
    rho = iota((512, 256), 1) & 127
    slot_mat = onehot(
        (shr(k, 4) == slot_lane) & ((shr(k, 1) & 7) == shr(rho, 4)) & ((k & 1) == (rho & 1))
    )
    row_block = shr(iota((128, 256), 0), 1) & 7
    row_level = jnp.zeros((128, 256), jnp.int32)
    for i in range(8):
        row_level = jnp.where(row_block == i, level[i], row_level)

    loads[2].wait()
    loads[3].wait()
    absorb_ends(1, fb)

    def column_copy(al, o):
        to = (gx + o) % NX
        return pltpu.make_async_remote_copy(
            src_ref=sbuf.at[al, to],
            dst_ref=rbuf.at[al, gx],
            send_sem=tsend.at[al],
            recv_sem=trecv.at[al],
            device_id=(gy, to),
            device_id_type=MESH,
        )

    for t in range(4):
        al = (t + 3) % 4
        absorb(1, fb, al)
        parts = []
        for b0 in (0, 4):
            v = mm(taps(fb, al, b0, 4), w2[...])
            v = v + fa[al + 1, 1 + b0 : 5 + b0, 1:9].reshape(512, 128).astype(F32)
            v = jnp.maximum(v, 0.0).astype(BF).reshape(4, 8, 16, 128)
            parts.append(
                jnp.concatenate([v[:, c].reshape(64, 128) for c in range(8)], axis=1)
            )
        rows = jnp.concatenate(parts, axis=0)
        lifted = jnp.zeros((128, 256), F32)
        for lv in range(4):
            lifted = jnp.where(row_level == lv, mm(rows, hw[lv]), lifted)
        high = lifted.astype(BF)
        low = (lifted - high.astype(F32)).astype(BF)
        sums = mm(slot_mat, jnp.concatenate([high, low], axis=0))
        sbuf[al] = sums.astype(BF).reshape(16, 32, 256)

        def send(o, c, al=al):
            column_copy(al, o).start()
            return c

        lax.fori_loop(1, NX, send, 0)
        rbuf[al, gx] = sbuf[al, gx]

    pltpu.make_async_copy(idl.at[0:15], idl.at[0:15], irecv).wait()
    sel = onehot(iota((128, 512), 0) == 2 * gx + (shr(iota((128, 512), 1), 4) & 1))
    got = mm(idl[...].reshape(16, 128).astype(BF), sel)
    got = jnp.where(iota((16, 512), 0) == shr(iota((16, 512), 1), 5), got, 0.0)
    cid = jnp.sum(got, axis=0, keepdims=True)
    r = iota((512, 512), 0)
    k = iota((512, 512), 1)
    want = (shr(r, 1) & 7) * 4 + shr(r, 7)
    tile_mat = onehot(
        (cid == want.astype(F32)) & ((shr(r, 4) & 7) == (shr(k, 1) & 7)) & ((r & 1) == (k & 1))
    )

    has_n = jnp.where(gy > 0, 1.0, 0.0).astype(F32)
    has_s = jnp.where(gy < NY - 1, 1.0, 0.0).astype(F32)
    has_w = jnp.where(gx > 0, 1.0, 0.0).astype(F32)
    has_e = jnp.where(gx < NX - 1, 1.0, 0.0).astype(F32)

    def rim(n, src, dst, where):
        return pltpu.make_async_remote_copy(
            src_ref=src,
            dst_ref=dst,
            send_sem=msend.at[n],
            recv_sem=mrecv.at[n],
            device_id=where,
            device_id_type=MESH,
        )

    early = [
        (can_w, can_e, rim(0, cstage.at[0, 0:3], cland.at[0, 0:3], (gy, west))),
        (can_e, can_w, rim(1, cstage.at[1, 0:3], cland.at[1, 0:3], (gy, east))),
        (can_n, can_s, rim(2, rstage.at[0], rland.at[0], (north, gx))),
        (can_n & can_w, can_s & can_e, rim(3, rstage.at[0, :, 0:16], kland.at[0], (north, west))),
        (can_n & can_e, can_s & can_w, rim(4, rstage.at[0, :, 16:32], kland.at[1], (north, east))),
    ]
    late = [
        (can_w, can_e, rim(5, cstage.at[0, 3:4], cland.at[0, 3:4], (gy, west))),
        (can_e, can_w, rim(6, cstage.at[1, 3:4], cland.at[1, 3:4], (gy, east))),
        (can_s, can_n, rim(7, rstage.at[1], rland.at[1], (south, gx))),
        (can_s & can_w, can_n & can_e, rim(8, rstage.at[1, :, 0:16], kland.at[2], (south, west))),
        (can_s & can_e, can_n & can_w, rim(9, rstage.at[1, :, 16:32], kland.at[3], (south, east))),
    ]
    rims = early + late

    def carry_down(arr, dst, src, x0, n):
        arr[dst, x0 : x0 + n] = one_down(arr[src, x0 : x0 + n], 0.0)

    def carry_up(arr, dst, src, x0, n):
        arr[dst, x0 : x0 + n] = one_up(arr[src, x0 : x0 + n], 0.0)

    def plane_inner(yl):
        win = [
            bev[yl + 1 + dy, 2 + dx : 32 + dx].reshape(480, 256)
            for dy in range(3)
            for dx in range(3)
        ]
        f = mm(jnp.concatenate(win, axis=1), p1[...])
        first[yl + 1, 2:32] = jnp.maximum(f, 0.0).astype(BF).reshape(30, 16, 256)

    for t in range(4):
        al = (t + 3) % 4
        pltpu.make_async_copy(rbuf.at[al, 0:15], rbuf.at[al, 0:15], trecv.at[al]).wait()
        tile = mm(tile_mat, rbuf[al].reshape(512, 256))
        bev[al + 2, 2:34] = tile.astype(BF).reshape(32, 16, 256)
        for c in range(2):
            cs = slice(128 * c, 128 * c + 128)
            tile32[c] = tile[:, cs]
            edge_rows = tile32[c, pl.ds(0 if al < 2 else 15, 32, stride=16), :]
            rstage[al // 2, al % 2, :, cs] = edge_rows.astype(BF)
        cstage[0, t] = bev[al + 2, 2:4]
        cstage[1, t] = bev[al + 2, 32:34]
        if t == 2:
            for to, back, c in early:
                pl.when(to)(c.start)
            loads[4].wait()
            carry_down(bev, 1, 5, 2, 32)
            plane_inner(0)
        if t == 3:
            for to, back, c in late:
                pl.when(to)(c.start)
            carry_up(bev, 6, 2, 2, 32)
            for yl in (3, 1, 2):
                plane_inner(yl)
            carry_down(first, 0, 4, 2, 30)
            carry_up(first, 5, 1, 2, 30)

    for to, back, c in rims:
        pl.when(back)(c.wait_recv)
    for t in range(4):
        al = (t + 3) % 4
        bev[al + 2, 34:36] = cland[0, t]
        bev[al + 2, 0:2] = cland[1, t]
    for x0 in (0, 34):
        carry_down(bev, 1, 5, x0, 2)
        carry_up(bev, 6, 2, x0, 2)
    for n in range(2):
        for c in range(2):
            cs = slice(128 * c, 128 * c + 128)
            for sub, way in ((0, 1), (15, 0)):
                rim32[n, c, pl.ds(32 + sub, 32, stride=16), :] = rland[way, n, :, cs].astype(F32)
                corner = kland[2 * way + 1, n, :, cs].astype(F32)[14:16]
                rim32[n, c, pl.ds(sub, 2, stride=16), :] = corner
                corner = kland[2 * way, n, :, cs].astype(F32)[0:2]
                rim32[n, c, pl.ds(544 + sub, 2, stride=16), :] = corner

    def map_half(slab, half):
        hs = slice(8 * half, 8 * half + 8)
        if slab in (0, 7):
            both = [rim32[slab // 7, c].reshape(36, 16, 128)[:, hs] for c in range(2)]
            return jnp.concatenate(both, axis=2)
        return bev[slab].astype(F32)[:, hs]

    s8 = iota((36, 8, 256), 1)
    for dy in range(3):
        top0, top1 = ((0, 7), (7, 2), (2, 3))[dy]
        low0, low1 = ((4, 5), (5, 0), (0, 7))[dy]
        here = map_half(top0, 0)
        after = pltpu.roll(map_half(top1, 0), 1, 1)
        upper = jnp.where(s8 == 0, here, jnp.where(s8 == 1, after, 0.0))
        here = map_half(low1, 1)
        before = pltpu.roll(map_half(low0, 1), 7, 1)
        lower = jnp.where(s8 == 7, here, jnp.where(s8 == 6, before, 0.0))
        bev[8 + dy] = jnp.concatenate([upper, lower], axis=1).astype(BF)
    win = [bev[8 + dy, dx : dx + 34].reshape(544, 256) for dy in range(3) for dx in range(3)]
    f = mm(jnp.concatenate(win, axis=1), p1[...])
    edge[...] = jnp.maximum(f, 0.0).reshape(34, 16, 256)
    win = [
        jnp.concatenate(
            [
                bev[1 + dy : 5 + dy, x0 + dx : x0 + dx + 2].reshape(128, 256) for x0 in (0, 32)
            ],
            axis=0,
        )
        for dy in range(3)
        for dx in range(3)
    ]
    f = mm(jnp.concatenate(win, axis=1), p1[...])
    f = jnp.maximum(f, 0.0).reshape(2, 4, 2, 16, 256)
    first[1:5, 0:1] = (f[0, :, 0:1] * has_w).astype(BF)
    first[1:5, 1:2] = f[0, :, 1:2].astype(BF)
    first[1:5, 32:33] = f[1, :, 0:1].astype(BF)
    first[1:5, 33:34] = (f[1, :, 1:2] * has_e).astype(BF)
    edge[0:1] = edge[0:1] * has_w
    edge[33:34] = edge[33:34] * has_e
    for x0 in (0, 32):
        carry_down(first, 0, 4, x0, 2)
        carry_up(first, 5, 1, x0, 2)
    s8 = iota((34, 8, 256), 1)
    upper = edge[:, 0:8]
    lower = edge[:, 8:16]

    def patch(slab, half, row, new):
        old = first[slab]
        keep = old[:, 0:8].astype(F32), old[:, 8:16].astype(F32)
        mixed = jnp.where(s8 == row, new, keep[half])
        both = [mixed, keep[1]] if half == 0 else [keep[0], mixed]
        first[slab] = jnp.concatenate(both, axis=1).astype(BF)

    patch(0, 0, 0, upper * has_n)
    patch(1, 0, 0, pltpu.roll(upper, 7, 1))
    patch(4, 1, 7, pltpu.roll(lower, 1, 1))
    patch(5, 1, 7, lower * has_s)
    base[...] = bev[2:6, 2:34]

    for ph in range(2):
        for way in range(2):
            ring(lambda ph=ph, way=way: end_copy(ph, way).wait_send(), way)
        for al in range(4):
            if ph == 1 or al in (1, 2):
                faces_sent(ph, al)
    for al in range(4):
        pltpu.make_async_copy(sbuf.at[al, 0:15], sbuf.at[al, 0:15], tsend.at[al]).wait()
    pltpu.make_async_copy(idl.at[0:15], idl.at[0:15], isend).wait()
    for to, back, c in rims:
        pl.when(to)(c.wait_send)


def last_kernel(first, base, p2, out, rows32, buf, sems):
    copies = []
    for yl in range(4):
        win = [
            first[yl + dy, dx : dx + 32].reshape(512, 256) for dy in range(3) for dx in range(3)
        ]
        s = mm(jnp.concatenate(win, axis=1), p2[...])
        s = s + base[yl].reshape(512, 256).astype(F32)
        for c in range(2):
            cs = slice(128 * c, 128 * c + 128)
            rows32[yl % 2, c] = s[:, cs]
            for y in range(16):
                buf[yl, y, :, cs] = rows32[yl % 2, c, pl.ds(y, 32, stride=16), :].astype(BF)
        c = pltpu.make_async_copy(buf.at[yl], out.at[:, yl], sems.at[yl])
        c.start()
        copies.append(c)
    for c in copies:
        c.wait()


def local(
    features, links, block_slot, block_level, slot_column,
    conv_first, conv_second, height_w, plane_first, plane_second,
):
    hbm = pl.BlockSpec(memory_space=pltpu.HBM)
    vmem = pl.BlockSpec(memory_space=pltpu.VMEM)
    dma = pltpu.SemaphoreType.DMA
    operands = (
        features.reshape(8, 2, 4, 64, 128),
        links.T,
        block_slot,
        block_level,
        slot_column,
        conv_first.reshape(896, 128),
        conv_second.reshape(896, 128),
        height_w,
        plane_first.reshape(2304, 256),
    )
    first, base = pl.pallas_call(
        kernel,
        out_shape=[
            jax.ShapeDtypeStruct((6, 34, 16, 256), BF),
            jax.ShapeDtypeStruct((4, 32, 16, 256), BF),
        ],
        in_specs=[hbm] * 9,
        out_specs=[vmem, vmem],
        scratch_shapes=[
            pltpu.SMEM((3, 8), jnp.int32),
            pltpu.SMEM((8,), jnp.int32),
            pltpu.SMEM((8,), jnp.int32),
            pltpu.VMEM((1, 32), jnp.int32),
            pltpu.VMEM((8, 2, 4, 64, 128), BF),
            pltpu.VMEM((896, 128), BF),
            pltpu.VMEM((896, 128), BF),
            pltpu.VMEM((4, 1024, 256), BF),
            pltpu.VMEM((2304, 256), BF),
            pltpu.VMEM((6, 10, 10, 16, 128), BF),
            pltpu.VMEM((6, 10, 10, 16, 128), BF),
            pltpu.VMEM((2, 2, 4, 2, 8, 16, 128), BF),
            pltpu.VMEM((2, 2, 4, 2, 8, 16, 128), BF),
            pltpu.VMEM((2, 2, 64, 128), BF),
            pltpu.VMEM((2, 2, 64, 128), BF),
            pltpu.VMEM((2, 1024, 128), F32),
            pltpu.VMEM((4, 16, 32, 256), BF),
            pltpu.VMEM((4, 16, 32, 256), BF),
            pltpu.VMEM((1, 128), F32),
            pltpu.VMEM((16, 1, 128), F32),
            pltpu.VMEM((11, 36, 16, 256), BF),
            pltpu.VMEM((34, 16, 256), F32),
            pltpu.VMEM((2, 512, 128), F32),
            pltpu.VMEM((2, 2, 576, 128), F32),
            pltpu.VMEM((2, 4, 2, 16, 256), BF),
            pltpu.VMEM((2, 4, 2, 16, 256), BF),
            pltpu.VMEM((2, 2, 32, 256), BF),
            pltpu.VMEM((2, 2, 32, 256), BF),
            pltpu.VMEM((4, 2, 16, 256), BF),
            dma((9,)),
            dma((2, 2, 4)),
            dma((2, 2, 4)),
            dma((2, 2)),
            dma((2, 2)),
            dma((4,)),
            dma((4,)),
            dma,
            dma,
            dma((10,)),
            dma((10,)),
        ],
        compiler_params=pltpu.CompilerParams(
            collective_id=0, has_side_effects=True, vmem_limit_bytes=40 * 2**20
        ),
    )(
        *[pltpu.with_memory_space_constraint(x, pltpu.HBM) for x in operands]
    )
    out = pl.pallas_call(
        last_kernel,
        out_shape=jax.ShapeDtypeStruct((16, 4, 32, 256), BF),
        in_specs=[vmem, vmem, vmem],
        out_specs=hbm,
        scratch_shapes=[
            pltpu.VMEM((2, 2, 512, 128), F32),
            pltpu.VMEM((4, 16, 32, 256), BF),
            dma((4,)),
        ],
        compiler_params=pltpu.CompilerParams(vmem_limit_bytes=24 * 2**20),
    )(first, base, plane_second.reshape(2304, 256))
    return out.reshape(64, 32, 256)


def solution(mesh):
    in_specs = (
        P(("gy", "gx"), None, None),
        P(("gy", "gx"), None),
        P(("gy", "gx")),
        P(("gy", "gx")),
        P(("gy", "gx"), None),
        P(),
        P(),
        P(),
        P(),
        P(),
    )
    return jax.shard_map(
        local, mesh=mesh, in_specs=in_specs, out_specs=P("gy", "gx", None), check_vma=False
    )
```

time: 51.9 us -> 45.4 us (0.87)
  Pallas kernels: 51.8 us -> 44.8 us
    pallas_call x1, Pallas kernels: 45.3 us -> 40.7 us  [local(): pl.pallas_call(kernel, out_shape=[jax.ShapeDtypeStruct((6, 34, 16, 256),...]
    pallas_call x1, Pallas kernels: 6.49 us -> 4.11 us  [local(): pl.pallas_call(last_kernel, out_shape=jax.ShapeDtypeStruct((16, 4, 32, 25...]
where the time goes in v3:
time: 45.4 us; the launch traced here: 45 us
  Pallas kernels  44.8 us (99%)
    pallas_call x1, Pallas kernels, local(): pl.pallas_call(kernel, out_shape=[jax.ShapeDtypeStruct((6, 34, 16, 256),...  40.7 us
    pallas_call x1, Pallas kernels, local(): pl.pallas_call(last_kernel, out_shape=jax.ShapeDtypeStruct((16, 4, 32, 25...  4.11 us

profile of v3, /device:TPU:1, one launch (start us, length us, event | category | flops | bytes accessed | tf_op | source)
XLA Modules:
  0.0 45.0 jit_solution(3940366629715936334)
XLA Ops:
  0.0 0.0 copy-start
  0.0 40.7 %shard_map.100 = (bf16[6,34,16,256]{3,2,1,0:T(8,128)(2,1)S(1)}, bf16[4,32,16,256]{3,2,1,0:T(8,128)(2,1)S(1)}) custom-call(bf16[8,2,4,64,128]{4,3,2,1,0:T(8,128)(2,1)} %bitcast.9, s32[3,8]{1,0:T(4,128)} %bitcast.12, s32[8]{0:T(128)} %slot_hbm.1, s32[8]{0:T(128)} %level_hbm.1, s32[1,32]{1,0:T(1,128)} %ids_hbm.1, bf16[896,128]{1,0:T(8,128)(2,1)} %bitcast.10, ...), custom_call_target="tpu_custom_call" | custom-call | tf_op jit(solution)/shard_map/pallas_call | solution.py:551
  40.7 0.0 copy-done
  40.7 4.1 %shard_map.101 = bf16[16,4,32,256]{3,2,1,0:T(8,128)(2,1)} custom-call(bf16[6,34,16,256]{3,2,1,0:T(8,128)(2,1)S(1)} %get-tuple-element.7.first, bf16[4,32,16,256]{3,2,1,0:T(8,128)(2,1)S(1)} %get-tuple-element.8.base, bf16[2304,256]{1,0:T(8,128)(2,1)S(1)} %bitcast.7), custom_call_target="tpu_custom_call" | custom-call | tf_op jit(solution)/shard_map/pallas_call | solution.py:607
Async XLA Ops:
  0.0 40.7 %copy-start = (bf16[3,3,256,256]{3,2,1,0:T(8,128)(2,1)S(1)}, bf16[3,3,256,256]{3,2,1,0:T(8,128)(2,1)}, u32[]{:S(2)}) copy-start(bf16[3,3,256,256]{3,2,1,0:T(8,128)(2,1)} %param.19) | copy-start | bytes 3538948

commit v4 on v3

--- a/solution.py
+++ b/solution.py
@@ -55,7 +55,7 @@
     links, slot, level, ids_in, xv, w1, w2, hw, p1,
     fa, fb, stage, ghost, astage, aghost,
     rows32, sbuf, rbuf, ids, idl,
-    bev, edge, tile32, rim32, cstage, cland, rstage, rland, kland,
+    bev, edge, win32, tile32, rim32, cstage, cland, rstage, rland, kland,
     wsem, hsend, hrecv, asend, arecv, tsend, trecv, isend, irecv, msend, mrecv,
 ):
     gy = lax.axis_index("gy")
@@ -69,7 +69,8 @@
         pltpu.make_async_copy(s, d, wsem.at[n])
         for n, (s, d) in enumerate(
             [
-                (x_hbm, xv), (w1_hbm, w1), (w2_hbm, w2), (h_hbm, hw), (p1_hbm, p1),
+                *[(x_hbm.at[:, :, al], xv.at[:, :, al]) for al in (3, 0, 1, 2)],
+                (w1_hbm, w1), (w2_hbm, w2), (h_hbm, hw), (p1_hbm, p1),
                 (links_hbm, links), (slot_hbm, slot), (level_hbm, level), (ids_hbm, ids_in),
             ]
         )
@@ -128,7 +129,7 @@
             for ref in land:
                 ref[...] = jnp.zeros(ref.shape, BF)
 
-    for load in loads[5:]:
+    for load in loads[8:]:
         load.wait()
     ids[...] = jnp.zeros((1, 128), F32)
     ids[0:1, 0:32] = ids_in[...].astype(F32)
@@ -221,7 +222,6 @@
         ]
         return jnp.concatenate([w.reshape(n, 128) for w in win], axis=1)
 
-    loads[0].wait()
 
     def send_ids(o, carry):
         pltpu.make_async_remote_copy(
@@ -234,28 +234,34 @@
         ).start()
         return carry
 
-    astage[0, 0] = xv[0, 0, 0]
-    astage[0, 1] = (xv[7, 1, 3].astype(F32) * top).astype(BF)
-    for t in range(4):
+    def bring(t):
         al = (t + 3) % 4
+        loads[t].wait()
         rows32[t % 2] = xv[:, :, al].reshape(1024, 128).astype(F32)
         for b in range(8):
             for c in range(8):
                 cell = rows32[t % 2, pl.ds(8 * b + c, 16, stride=64), :]
                 fa[al + 1, 1 + b, 1 + c] = cell.astype(BF)
         lay_out(0, fa, al)
-    idl[gx] = ids[...]
+
+    bring(0)
+    astage[0, 1] = (xv[7, 1, 3].astype(F32) * top).astype(BF)
+    bring(1)
+    astage[0, 0] = xv[0, 0, 0]
     pl.semaphore_wait(barrier, greeted)
     send_end(0, 0)
     send_end(0, 1)
     send_faces(0, 3)
     send_faces(0, 0)
+    bring(2)
+    bring(3)
+    idl[gx] = ids[...]
     faces_sent(0, 3)
     send_faces(0, 1)
     faces_sent(0, 0)
     send_faces(0, 2)
 
-    loads[1].wait()
+    loads[4].wait()
     absorb_ends(0, fa)
 
     for t in range(4):
@@ -292,8 +298,8 @@
     for i in range(8):
         row_level = jnp.where(row_block == i, level[i], row_level)
 
-    loads[2].wait()
-    loads[3].wait()
+    loads[5].wait()
+    loads[6].wait()
     absorb_ends(1, fb)
 
     def column_copy(al, o):
@@ -407,7 +413,7 @@
         if t == 2:
             for to, back, c in early:
                 pl.when(to)(c.start)
-            loads[4].wait()
+            loads[7].wait()
             carry_down(bev, 1, 5, 2, 32)
             plane_inner(0)
         if t == 3:
@@ -449,16 +455,14 @@
     for dy in range(3):
         top0, top1 = ((0, 7), (7, 2), (2, 3))[dy]
         low0, low1 = ((4, 5), (5, 0), (0, 7))[dy]
-        here = map_half(top0, 0)
-        after = pltpu.roll(map_half(top1, 0), 1, 1)
-        upper = jnp.where(s8 == 0, here, jnp.where(s8 == 1, after, 0.0))
-        here = map_half(low1, 1)
-        before = pltpu.roll(map_half(low0, 1), 7, 1)
-        lower = jnp.where(s8 == 7, here, jnp.where(s8 == 6, before, 0.0))
-        bev[8 + dy] = jnp.concatenate([upper, lower], axis=1).astype(BF)
-    win = [bev[8 + dy, dx : dx + 34].reshape(544, 256) for dy in range(3) for dx in range(3)]
+        upper = jnp.where(s8 == 0, map_half(top0, 0), pltpu.roll(map_half(top1, 0), 1, 1))
+        lower = jnp.where(s8 == 7, map_half(low1, 1), pltpu.roll(map_half(low0, 1), 7, 1))
+        win32[dy] = jnp.where(s8 < 2, upper, jnp.where(s8 > 5, lower, 0.0))
+    win = [
+        win32[dy, dx : dx + 34].reshape(272, 256).astype(BF) for dy in range(3) for dx in range(3)
+    ]
     f = mm(jnp.concatenate(win, axis=1), p1[...])
-    edge[...] = jnp.maximum(f, 0.0).reshape(34, 16, 256)
+    edge[...] = jnp.maximum(f, 0.0).reshape(34, 8, 256)
     win = [
         jnp.concatenate(
             [
@@ -481,8 +485,7 @@
         carry_down(first, 0, 4, x0, 2)
         carry_up(first, 5, 1, x0, 2)
     s8 = iota((34, 8, 256), 1)
-    upper = edge[:, 0:8]
-    lower = edge[:, 8:16]
+    rows = edge[...]
 
     def patch(slab, half, row, new):
         old = first[slab]
@@ -491,10 +494,10 @@
         both = [mixed, keep[1]] if half == 0 else [keep[0], mixed]
         first[slab] = jnp.concatenate(both, axis=1).astype(BF)
 
-    patch(0, 0, 0, upper * has_n)
-    patch(1, 0, 0, pltpu.roll(upper, 7, 1))
-    patch(4, 1, 7, pltpu.roll(lower, 1, 1))
-    patch(5, 1, 7, lower * has_s)
+    patch(0, 0, 0, rows * has_n)
+    patch(1, 0, 0, pltpu.roll(rows, 7, 1))
+    patch(4, 1, 7, pltpu.roll(rows, 1, 1))
+    patch(5, 1, 7, rows * has_s)
     base[...] = bev[2:6, 2:34]
 
     for ph in range(2):
@@ -512,18 +515,21 @@
 
 def last_kernel(first, base, p2, out, rows32, buf, sems):
     copies = []
-    for yl in range(4):
+    for n, (yl, x0, m) in enumerate(((0, 0, 32), (1, 0, 32), (2, 0, 32), (3, 0, 16), (3, 16, 16))):
+        xs = slice(x0, x0 + m)
         win = [
-            first[yl + dy, dx : dx + 32].reshape(512, 256) for dy in range(3) for dx in range(3)
+            first[yl + dy, x0 + dx : x0 + dx + m].reshape(16 * m, 256)
+            for dy in range(3)
+            for dx in range(3)
         ]
         s = mm(jnp.concatenate(win, axis=1), p2[...])
-        s = s + base[yl].reshape(512, 256).astype(F32)
+        s = s + base[yl, xs].reshape(16 * m, 256).astype(F32)
         for c in range(2):
             cs = slice(128 * c, 128 * c + 128)
-            rows32[yl % 2, c] = s[:, cs]
+            rows32[n % 2, c, 0 : 16 * m] = s[:, cs]
             for y in range(16):
-                buf[yl, y, :, cs] = rows32[yl % 2, c, pl.ds(y, 32, stride=16), :].astype(BF)
-        c = pltpu.make_async_copy(buf.at[yl], out.at[:, yl], sems.at[yl])
+                buf[yl, y, xs, cs] = rows32[n % 2, c, pl.ds(y, m, stride=16), :].astype(BF)
+        c = pltpu.make_async_copy(buf.at[yl, :, xs], out.at[:, yl, xs], sems.at[n])
         c.start()
         copies.append(c)
     for c in copies:
@@ -577,8 +583,9 @@
             pltpu.VMEM((4, 16, 32, 256), BF),
             pltpu.VMEM((1, 128), F32),
             pltpu.VMEM((16, 1, 128), F32),
-            pltpu.VMEM((11, 36, 16, 256), BF),
-            pltpu.VMEM((34, 16, 256), F32),
+            pltpu.VMEM((7, 36, 16, 256), BF),
+            pltpu.VMEM((34, 8, 256), F32),
+            pltpu.VMEM((3, 36, 8, 256), F32),
             pltpu.VMEM((2, 512, 128), F32),
             pltpu.VMEM((2, 2, 576, 128), F32),
             pltpu.VMEM((2, 4, 2, 16, 256), BF),
@@ -586,7 +593,7 @@
             pltpu.VMEM((2, 2, 32, 256), BF),
             pltpu.VMEM((2, 2, 32, 256), BF),
             pltpu.VMEM((4, 2, 16, 256), BF),
-            dma((9,)),
+            dma((12,)),
             dma((2, 2, 4)),
             dma((2, 2, 4)),
             dma((2, 2)),
@@ -612,7 +619,7 @@
         scratch_shapes=[
             pltpu.VMEM((2, 2, 512, 128), F32),
             pltpu.VMEM((4, 16, 32, 256), BF),
-            dma((4,)),
+            dma((5,)),
         ],
         compiler_params=pltpu.CompilerParams(vmem_limit_bytes=24 * 2**20),
     )(first, base, plane_second.reshape(2304, 256))

time: 45.4 us -> 44.5 us (0.980)
  Pallas kernels: 44.8 us -> 44.2 us
    pallas_call x1, Pallas kernels: 40.7 us -> 40.1 us  [local(): pl.pallas_call(kernel, out_shape=[jax.ShapeDtypeStruct((6, 34, 16, 256),...]
where the time goes in v4:
time: 44.5 us; the launch traced here: 44.4 us
  Pallas kernels  44.2 us (99%)
    pallas_call x1, Pallas kernels, local(): pl.pallas_call(kernel, out_shape=[jax.ShapeDtypeStruct((6, 34, 16, 256),...  40.1 us
    pallas_call x1, Pallas kernels, local(): pl.pallas_call(last_kernel, out_shape=jax.ShapeDtypeStruct((16, 4, 32, 25...  4.12 us

profile of v4, /device:TPU:1, one launch (start us, length us, event | category | flops | bytes accessed | tf_op | source)
XLA Modules:
  0.0 44.4 jit_solution(6984041331170677940)
XLA Ops:
  0.0 0.0 copy-start
  0.0 40.1 %shard_map.100 = (bf16[6,34,16,256]{3,2,1,0:T(8,128)(2,1)S(1)}, bf16[4,32,16,256]{3,2,1,0:T(8,128)(2,1)S(1)}) custom-call(bf16[8,2,4,64,128]{4,3,2,1,0:T(8,128)(2,1)} %bitcast.9, s32[3,8]{1,0:T(4,128)} %bitcast.12, s32[8]{0:T(128)} %slot_hbm.1, s32[8]{0:T(128)} %level_hbm.1, s32[1,32]{1,0:T(1,128)} %ids_hbm.1, bf16[896,128]{1,0:T(8,128)(2,1)} %bitcast.10, ...), custom_call_target="tpu_custom_call" | custom-call | tf_op jit(solution)/shard_map/pallas_call | solution.py:557
  40.1 0.0 copy-done
  40.1 4.1 %shard_map.101 = bf16[16,4,32,256]{3,2,1,0:T(8,128)(2,1)} custom-call(bf16[6,34,16,256]{3,2,1,0:T(8,128)(2,1)S(1)} %get-tuple-element.7.first, bf16[4,32,16,256]{3,2,1,0:T(8,128)(2,1)S(1)} %get-tuple-element.8.base, bf16[2304,256]{1,0:T(8,128)(2,1)S(1)} %bitcast.7), custom_call_target="tpu_custom_call" | custom-call | tf_op jit(solution)/shard_map/pallas_call | solution.py:614
Async XLA Ops:
  0.0 40.1 %copy-start = (bf16[3,3,256,256]{3,2,1,0:T(8,128)(2,1)S(1)}, bf16[3,3,256,256]{3,2,1,0:T(8,128)(2,1)}, u32[]{:S(2)}) copy-start(bf16[3,3,256,256]{3,2,1,0:T(8,128)(2,1)} %param.19) | copy-start | bytes 3538948

commit v5 on v4

--- a/solution.py
+++ b/solution.py
@@ -199,15 +199,16 @@
         arr[al + 1, 0, 1:9] = ghost[ph, 1, al, 0]
         arr[al + 1, 1:9, 0] = ghost[ph, 1, al, 1]
 
-    def absorb_ends(ph, arr):
-        for way in range(2):
-            ring(lambda way=way: end_copy(ph, way).wait_recv(), way, True)
-        rows32[0, pl.ds(15, 64, stride=16), :] = aghost[ph, 0].astype(F32) * top
-        rows32[0, pl.ds(0, 64, stride=16), :] = aghost[ph, 1].astype(F32)
+    def absorb_end(ph, arr, way):
+        ring(lambda: end_copy(ph, way).wait_recv(), way, True)
+        come = aghost[ph, way].astype(F32)
+        rows32[way, pl.ds(0 if way else 15, 64, stride=16), :] = come if way else come * top
         for b in range(8):
-            low, high = halves(rows32[0, b * 128 : b * 128 + 128].reshape(8, 16, 128))
-            arr[5, 1 + b, 1:9] = one_up(arr[1, 1 + b, 1:9], high, (ma[0:8], ma[8:16]))
-            arr[0, 1 + b, 1:9] = one_down(arr[4, 1 + b, 1:9], low, (mb[0:8], mb[8:16]))
+            low, high = halves(rows32[way, b * 128 : b * 128 + 128].reshape(8, 16, 128))
+            if way:
+                arr[0, 1 + b, 1:9] = one_down(arr[4, 1 + b, 1:9], low, (mb[0:8], mb[8:16]))
+            else:
+                arr[5, 1 + b, 1:9] = one_up(arr[1, 1 + b, 1:9], high, (ma[0:8], ma[8:16]))
 
     def taps(arr, al, b0, nb):
         n = nb * 128
@@ -262,7 +263,8 @@
     send_faces(0, 2)
 
     loads[4].wait()
-    absorb_ends(0, fa)
+    absorb_end(0, fa, 0)
+    absorb_end(0, fa, 1)
 
     for t in range(4):
         al = (t + 3) % 4
@@ -300,7 +302,6 @@
 
     loads[5].wait()
     loads[6].wait()
-    absorb_ends(1, fb)
 
     def column_copy(al, o):
         to = (gx + o) % NX
@@ -315,6 +316,8 @@
 
     for t in range(4):
         al = (t + 3) % 4
+        if t < 2:
+            absorb_end(1, fb, t)
         absorb(1, fb, al)
         parts = []
         for b0 in (0, 4):

time: 44.5 us -> 44.5 us (level)
  no operation moved by 1% of the time
where the time goes in v5:
time: 44.5 us; the launch traced here: 44.3 us
  Pallas kernels  44.1 us (99%)
    pallas_call x1, Pallas kernels, local(): pl.pallas_call(kernel, out_shape=[jax.ShapeDtypeStruct((6, 34, 16, 256),...  40 us
    pallas_call x1, Pallas kernels, local(): pl.pallas_call(last_kernel, out_shape=jax.ShapeDtypeStruct((16, 4, 32, 25...  4.12 us

profile of v5, /device:TPU:1, one launch (start us, length us, event | category | flops | bytes accessed | tf_op | source)
XLA Modules:
  0.0 44.3 jit_solution(10625987942580198479)
XLA Ops:
  0.0 0.0 copy-start
  0.0 40.0 %shard_map.100 = (bf16[6,34,16,256]{3,2,1,0:T(8,128)(2,1)S(1)}, bf16[4,32,16,256]{3,2,1,0:T(8,128)(2,1)S(1)}) custom-call(bf16[8,2,4,64,128]{4,3,2,1,0:T(8,128)(2,1)} %bitcast.9, s32[3,8]{1,0:T(4,128)} %bitcast.12, s32[8]{0:T(128)} %slot_hbm.1, s32[8]{0:T(128)} %level_hbm.1, s32[1,32]{1,0:T(1,128)} %ids_hbm.1, bf16[896,128]{1,0:T(8,128)(2,1)} %bitcast.10, ...), custom_call_target="tpu_custom_call" | custom-call | tf_op jit(solution)/shard_map/pallas_call | solution.py:560
  40.0 0.0 copy-done
  40.0 4.1 %shard_map.101 = bf16[16,4,32,256]{3,2,1,0:T(8,128)(2,1)} custom-call(bf16[6,34,16,256]{3,2,1,0:T(8,128)(2,1)S(1)} %get-tuple-element.7.first, bf16[4,32,16,256]{3,2,1,0:T(8,128)(2,1)S(1)} %get-tuple-element.8.base, bf16[2304,256]{1,0:T(8,128)(2,1)S(1)} %bitcast.7), custom_call_target="tpu_custom_call" | custom-call | tf_op jit(solution)/shard_map/pallas_call | solution.py:617
Async XLA Ops:
  0.0 40.0 %copy-start = (bf16[3,3,256,256]{3,2,1,0:T(8,128)(2,1)S(1)}, bf16[3,3,256,256]{3,2,1,0:T(8,128)(2,1)}, u32[]{:S(2)}) copy-start(bf16[3,3,256,256]{3,2,1,0:T(8,128)(2,1)} %param.19) | copy-start | bytes 3538948
